TPU v7x, 32 devices: a whole 2x2x4 slice. The times are simulated.
32 devices in a mesh: dp: 8 (over z, y), mp: 4 (over x, core).
Axes of the slice: x: 2, y: 2, z: 4, core: 2. Of those that a mesh axis runs over, the one named last changes fastest.
Arguments:
- tokens: bfloat16 [4096, 1152], P(('dp', 'mp')), may hold values from -6 to 6
- segment_ids: int32 [4096], P('dp'), may hold values from 0 to 2, as said below
- positions: int32 [4096], P('dp'), may hold values from 0 to 5118, as said below
- q_weight: bfloat16 [1152, 1024], P('dp', 'mp'), may hold values from -0.1875 to 0.1875
- kv_weight: bfloat16 [1152, 512], P('dp'), may hold values from -0.1875 to 0.1875
- o_weight: bfloat16 [1024, 1152], P('mp', 'dp'), may hold values from -0.1875 to 0.1875
- gate_up_weight: bfloat16 [2, 1152, 6912], P(None, 'dp', 'mp'), may hold values from -0.1875 to 0.1875
- down_weight: bfloat16 [6912, 1152], P('mp', 'dp'), may hold values from -0.078125 to 0.078125
- attn_pre_gain: bfloat16 [1152], P('dp'), may hold values from 0.25 to 1.75
- attn_post_gain: bfloat16 [1152], P('dp'), may hold values from 0.25 to 1.75
- ff_pre_gain: bfloat16 [1152], P('dp'), may hold values from 0.25 to 1.75
- ff_post_gain: bfloat16 [1152], P('dp'), may hold values from 0.25 to 1.75
- query_gain: bfloat16 [256], P('dp'), may hold values from 0.25 to 1.75
- key_gain: bfloat16 [256], P('dp'), may hold values from 0.25 to 1.75
- out_grad: bfloat16 [4096, 1152], P(('dp', 'mp')), may hold values from -6 to 6
Outputs:
- out: bfloat16 [4096, 1152], P(('dp', 'mp'))
- tokens_grad: float32 [4096, 1152], P(('dp', 'mp'))
- q_weight_grad: float32 [1152, 1024], P('dp', 'mp')
- kv_weight_grad: float32 [1152, 512], P('dp')
- o_weight_grad: float32 [1024, 1152], P('mp', 'dp')
- gate_up_weight_grad: float32 [2, 1152, 6912], P(None, 'dp', 'mp')
- down_weight_grad: float32 [6912, 1152], P('mp', 'dp')
- attn_pre_gain_grad: float32 [1152], P('dp')
- attn_post_gain_grad: float32 [1152], P('dp')
- ff_pre_gain_grad: float32 [1152], P('dp')
- ff_post_gain_grad: float32 [1152], P('dp')
- query_gain_grad: float32 [256], P('dp')
- key_gain_grad: float32 [256], P('dp')
Inputs may be any that keep to these rules, and one draw needn't show every extreme that they name: `segment_ids`: segment ids never fall; document 0 and document 2 each hold 1 to 256 tokens, document 1 the rest. Within a document, positions rise by one from token to token; document 0 starts at position 0, document 2 at 0 to 1023, and the last token of document 1 has position 5118.
All inputs are finite; a program needn't handle non-finite values.
Results may differ from a plain program's by a relative error of at most 0.028.
Values may be sent and summed in bfloat16 or wider, within the bound.
A program may use at most 128 MiB of HBM per device.

v0:
```python
from functools import partial

import jax
import jax.numpy as jnp
from jax import lax
from jax.sharding import PartitionSpec as P

WINDOW = 512


EPS = 1e-06
NEG = -1e30


def from_behind(value, axis, steps):
    count = lax.axis_size(axis)
    leading, last = (max(0, -steps), min(count, count - steps))
    return lax.ppermute(value, axis, [(source, source + steps) for source in range(leading, last)])


def normalize(value, gain):
    return value * lax.rsqrt(jnp.mean(value * value, axis=-1, keepdims=True) + EPS) * gain


def rotary_tables(positions, width):
    half_width = width // 2
    frequency = jnp.power(10000.0, -jnp.arange(half_width, dtype=jnp.float32) * (2.0 / width))
    angles = positions.astype(jnp.float32)[:, None] * frequency[None, :]
    return (jnp.cos(angles), jnp.sin(angles))


def rotate(value, cosine, sine):
    half_width = value.shape[-1] // 2
    first_half = value[..., :half_width]
    second_half = value[..., half_width:]
    return jnp.concatenate(
        [first_half * cosine - second_half * sine, second_half * cosine + first_half * sine],
        axis=-1,
    )


def prepare_head(pre_value, gain, cosine, sine):
    return rotate(normalize(pre_value, gain), cosine, sine)


def gated_units(gate, up_part):
    return jax.nn.gelu(gate, approximate=True) * up_part


def norm_back(value, gain, grad):
    unused, pull = jax.vjp(normalize, value, gain)
    return pull(grad)


def local(
    tokens,
    segment_ids,
    positions,
    q_weight,
    kv_weight,
    o_weight,
    gate_up_weight,
    down_weight,
    attn_pre_gain,
    attn_post_gain,
    ff_pre_gain,
    ff_post_gain,
    query_gain,
    key_gain,
    out_grad,
):
    whole = (
        lax.all_gather(q_weight, "dp", axis=0, tiled=True),
        lax.all_gather(kv_weight, "dp", axis=0, tiled=True),
        lax.all_gather(o_weight, "dp", axis=1, tiled=True),
        lax.all_gather(gate_up_weight, "dp", axis=1, tiled=True),
        lax.all_gather(down_weight, "dp", axis=1, tiled=True),
        lax.all_gather(attn_pre_gain, "dp", axis=0, tiled=True),
        lax.all_gather(attn_post_gain, "dp", axis=0, tiled=True),
        lax.all_gather(ff_pre_gain, "dp", axis=0, tiled=True),
        lax.all_gather(ff_post_gain, "dp", axis=0, tiled=True),
        lax.all_gather(query_gain, "dp", axis=0, tiled=True),
        lax.all_gather(key_gain, "dp", axis=0, tiled=True),
    )
    query_full, keyval_full, output_full, gate_up_full, down_full = (
        whole[0],
        whole[1],
        whole[2],
        whole[3],
        whole[4],
    )
    gains = [item.astype(jnp.float32) for item in whole[5:]]
    head_size = query_full.shape[1]
    length = segment_ids.shape[0]
    reach = -(-WINDOW // length)
    block_size = min(512, length)
    score_scale = head_size ** (-0.5)
    span = block_size + WINDOW
    cosine, sine = rotary_tables(positions, head_size)
    distance = (
        jnp.arange(block_size, dtype=jnp.int32)[:, None]
        + WINDOW
        - jnp.arange(span, dtype=jnp.int32)[None, :]
    )
    inside = (distance >= 0) & (distance < WINDOW)
    residual = tokens.astype(jnp.float32)
    attn_local = normalize(residual, gains[0]).astype(jnp.bfloat16)
    attn_in = lax.all_gather(attn_local, "mp", axis=0, tiled=True)
    joint_weight = jnp.concatenate([query_full, keyval_full], axis=1)
    projected = jnp.dot(attn_in, joint_weight, preferred_element_type=jnp.float32)
    query_pre = projected[:, :head_size]
    key_pre = projected[:, head_size : 2 * head_size]
    value_pre = projected[:, 2 * head_size :]
    queries = prepare_head(query_pre, gains[4], cosine, sine).astype(jnp.bfloat16)
    keys = prepare_head(key_pre, gains[5], cosine, sine).astype(jnp.bfloat16)
    values = value_pre.astype(jnp.bfloat16)
    marks = (segment_ids + 1).astype(jnp.bfloat16)
    key_parts, value_parts, mark_parts = ([], [], [])
    step = 1
    moved = from_behind((keys, values, marks), "dp", step)
    key_parts.append(moved[0])
    value_parts.append(moved[1])
    mark_parts.append(moved[2])
    all_keys = jnp.concatenate(key_parts + [keys], axis=0)
    all_values = jnp.concatenate(value_parts + [values], axis=0)
    all_marks = jnp.concatenate(mark_parts + [marks], axis=0)

    def block_parts(start):
        first_key = start + reach * length - WINDOW
        visible = inside & (marks[:, None] == all_marks[None, :])
        product = (
            jnp.einsum("qd,kd->qk", queries, all_keys, preferred_element_type=jnp.float32)
            * score_scale
        )
        return (first_key, queries, all_keys, all_values, jnp.where(visible, product, NEG))

    mixed_parts, total_parts = ([], [])
    start = 0
    first_key, query_block, key_block, value_block, scores = block_parts(start)
    highest = jnp.max(scores, axis=-1, keepdims=True)
    expo = jnp.exp(scores - highest)
    denominator = jnp.sum(expo, axis=-1, keepdims=True)
    probs = (expo / denominator).astype(jnp.bfloat16)
    mixed_parts.append(jnp.dot(probs, value_block, preferred_element_type=jnp.float32))
    total_parts.append(highest + jnp.log(denominator))
    attended = mixed_parts[0].astype(jnp.bfloat16)
    log_totals = total_parts[0]
    attn_out = lax.psum_scatter(
        jnp.dot(attended, output_full, preferred_element_type=jnp.float32),
        "mp",
        scatter_dimension=0,
        tiled=True,
    )
    middle = residual + normalize(attn_out, gains[1])
    ff_local = normalize(middle, gains[2]).astype(jnp.bfloat16)
    ff_in = lax.all_gather(ff_local, "mp", axis=0, tiled=True)
    gate = jnp.dot(ff_in, gate_up_full[0], preferred_element_type=jnp.float32)
    up_part = jnp.dot(ff_in, gate_up_full[1], preferred_element_type=jnp.float32)
    hidden = gated_units(gate, up_part).astype(jnp.bfloat16)
    ff_out = lax.psum_scatter(
        jnp.dot(hidden, down_full, preferred_element_type=jnp.float32).astype(jnp.bfloat16),
        "mp",
        scatter_dimension=0,
        tiled=True,
    ).astype(jnp.float32)
    result = (middle + normalize(ff_out, gains[3])).astype(jnp.bfloat16)
    again = (
        lax.all_gather(q_weight, "dp", axis=0, tiled=True),
        lax.all_gather(kv_weight, "dp", axis=0, tiled=True),
        lax.all_gather(o_weight, "dp", axis=1, tiled=True),
        lax.all_gather(gate_up_weight, "dp", axis=1, tiled=True),
        lax.all_gather(down_weight, "dp", axis=1, tiled=True),
        lax.all_gather(attn_pre_gain, "dp", axis=0, tiled=True),
        lax.all_gather(attn_post_gain, "dp", axis=0, tiled=True),
        lax.all_gather(ff_pre_gain, "dp", axis=0, tiled=True),
        lax.all_gather(ff_post_gain, "dp", axis=0, tiled=True),
        lax.all_gather(query_gain, "dp", axis=0, tiled=True),
        lax.all_gather(key_gain, "dp", axis=0, tiled=True),
    )
    query_back, keyval_back, output_back, gate_up_back, down_back = (
        again[0],
        again[1],
        again[2],
        again[3],
        again[4],
    )
    gains_back = [item.astype(jnp.float32) for item in again[5:]]
    top_grad = out_grad.astype(jnp.float32)
    ff_out_grad, ff_post_grad = norm_back(ff_out, gains_back[3], top_grad)
    ff_grad_all = lax.all_gather(ff_out_grad.astype(jnp.bfloat16), "mp", axis=0, tiled=True)
    hidden_grad = jnp.einsum(
        "ld,fd->lf", ff_grad_all, down_back, preferred_element_type=jnp.float32
    )
    down_grad_turned = jnp.einsum(
        "ld,lf->df", ff_grad_all, hidden, preferred_element_type=jnp.float32
    )
    unused, unit_pull = jax.vjp(gated_units, gate, up_part)
    gate_grad, up_grad = unit_pull(hidden_grad)
    gate_low = gate_grad.astype(jnp.bfloat16)
    up_low = up_grad.astype(jnp.bfloat16)
    gate_up_turned = jnp.stack(
        [
            jnp.einsum("ld,lf->df", ff_in, gate_low, preferred_element_type=jnp.float32),
            jnp.einsum("ld,lf->df", ff_in, up_low, preferred_element_type=jnp.float32),
        ],
        axis=1,
    )
    ff_in_grad = lax.psum_scatter(
        (
            jnp.einsum("lf,df->ld", gate_low, gate_up_back[0], preferred_element_type=jnp.float32)
            + jnp.einsum("lf,df->ld", up_low, gate_up_back[1], preferred_element_type=jnp.float32)
        ).astype(jnp.bfloat16),
        "mp",
        scatter_dimension=0,
        tiled=True,
    ).astype(jnp.float32)
    middle_part, ff_pre_grad = norm_back(middle, gains_back[2], ff_in_grad)
    middle_grad = top_grad + middle_part
    attn_out_grad, attn_post_grad = norm_back(attn_out, gains_back[1], middle_grad)
    attn_grad_all = lax.all_gather(attn_out_grad.astype(jnp.bfloat16), "mp", axis=0, tiled=True)
    attended_grad = jnp.einsum(
        "ld,ed->le", attn_grad_all, output_back, preferred_element_type=jnp.float32
    ).astype(jnp.bfloat16)
    output_grad_turned = jnp.einsum(
        "ld,le->de", attn_grad_all, attended, preferred_element_type=jnp.float32
    )
    key_grad_all = jnp.zeros(((reach + 1) * length, head_size), jnp.float32)
    value_grad_all = jnp.zeros(((reach + 1) * length, head_size), jnp.float32)
    start = 0
    first_key, query_block, key_block, value_block, scores = block_parts(start)
    probs = jnp.exp(scores - log_totals)
    probs_low = probs.astype(jnp.bfloat16)
    value_grad_all = value_grad_all.at[first_key : first_key + span].add(
        jnp.einsum("qk,qd->kd", probs_low, attended_grad, preferred_element_type=jnp.float32)
    )
    prob_grad = jnp.einsum(
        "qd,kd->qk", attended_grad, value_block, preferred_element_type=jnp.float32
    )
    inner = jnp.sum(probs * prob_grad, axis=-1, keepdims=True)
    score_grad = (probs * (prob_grad - inner)).astype(jnp.bfloat16)
    query_parts = jnp.dot(score_grad, key_block, preferred_element_type=jnp.float32) * score_scale
    key_grad_all = key_grad_all.at[first_key : first_key + span].add(
        jnp.einsum("qk,qd->kd", score_grad, query_block, preferred_element_type=jnp.float32)
        * score_scale
    )
    own_keys = key_grad_all[reach * length :]
    own_values = value_grad_all[reach * length :]
    step = 1
    slot = reach - step
    returned = (
        from_behind(
            key_grad_all[slot * length : (slot + 1) * length].astype(jnp.bfloat16), "dp", -step
        ).astype(jnp.float32),
        from_behind(
            value_grad_all[slot * length : (slot + 1) * length].astype(jnp.bfloat16), "dp", -step
        ).astype(jnp.float32),
    )
    own_keys = own_keys + returned[0]
    own_values = own_values + returned[1]
    unused, query_pull = jax.vjp(
        partial(prepare_head, cosine=cosine, sine=sine), query_pre, gains_back[4]
    )
    query_pre_grad, query_gain_grad = query_pull(query_parts)
    unused, key_pull = jax.vjp(
        partial(prepare_head, cosine=cosine, sine=sine), key_pre, gains_back[5]
    )
    key_pre_grad, key_gain_grad = key_pull(own_keys)
    joint_grad_rows = jnp.concatenate([query_pre_grad, key_pre_grad, own_values], axis=1).astype(
        jnp.bfloat16
    )
    joint_back = jnp.concatenate([query_back, keyval_back], axis=1)
    joint_grad = jnp.einsum(
        "ld,lc->dc", attn_in, joint_grad_rows, preferred_element_type=jnp.float32
    )
    attn_in_grad = lax.psum_scatter(
        jnp.einsum(
            "lc,dc->ld", joint_grad_rows, joint_back, preferred_element_type=jnp.float32
        ).astype(jnp.bfloat16),
        "mp",
        scatter_dimension=0,
        tiled=True,
    ).astype(jnp.float32)
    tokens_part, attn_pre_grad = norm_back(residual, gains_back[0], attn_in_grad)
    tokens_grad = middle_grad + tokens_part
    owned = (
        lax.psum_scatter(
            joint_grad[:, :head_size].astype(jnp.bfloat16), "dp", scatter_dimension=0, tiled=True
        ).astype(jnp.float32),
        lax.psum_scatter(
            joint_grad[:, head_size:].astype(jnp.bfloat16), "dp", scatter_dimension=0, tiled=True
        ).astype(jnp.float32),
        lax.psum_scatter(
            output_grad_turned.astype(jnp.bfloat16), "dp", scatter_dimension=0, tiled=True
        ).astype(jnp.float32),
        lax.psum_scatter(
            gate_up_turned.astype(jnp.bfloat16), "dp", scatter_dimension=0, tiled=True
        ).astype(jnp.float32),
        lax.psum_scatter(
            down_grad_turned.astype(jnp.bfloat16), "dp", scatter_dimension=0, tiled=True
        ).astype(jnp.float32),
        lax.psum_scatter(
            attn_pre_grad.astype(jnp.bfloat16), "dp", scatter_dimension=0, tiled=True
        ).astype(jnp.float32),
        lax.psum_scatter(
            attn_post_grad.astype(jnp.bfloat16), "dp", scatter_dimension=0, tiled=True
        ).astype(jnp.float32),
        lax.psum_scatter(
            ff_pre_grad.astype(jnp.bfloat16), "dp", scatter_dimension=0, tiled=True
        ).astype(jnp.float32),
        lax.psum_scatter(
            ff_post_grad.astype(jnp.bfloat16), "dp", scatter_dimension=0, tiled=True
        ).astype(jnp.float32),
        lax.psum_scatter(
            query_gain_grad.astype(jnp.bfloat16), "dp", scatter_dimension=0, tiled=True
        ).astype(jnp.float32),
        lax.psum_scatter(
            key_gain_grad.astype(jnp.bfloat16), "dp", scatter_dimension=0, tiled=True
        ).astype(jnp.float32),
    )
    output_owned = jnp.transpose(owned[2])
    gate_up_owned = jnp.transpose(owned[3], (1, 0, 2))
    down_owned = jnp.transpose(owned[4])
    shared = (
        lax.psum(owned[1].astype(jnp.bfloat16), "mp").astype(jnp.float32),
        lax.psum(owned[5].astype(jnp.bfloat16), "mp").astype(jnp.float32),
        lax.psum(owned[6].astype(jnp.bfloat16), "mp").astype(jnp.float32),
        lax.psum(owned[7].astype(jnp.bfloat16), "mp").astype(jnp.float32),
        lax.psum(owned[8].astype(jnp.bfloat16), "mp").astype(jnp.float32),
        lax.psum(owned[9].astype(jnp.bfloat16), "mp").astype(jnp.float32),
        lax.psum(owned[10].astype(jnp.bfloat16), "mp").astype(jnp.float32),
    )
    return (
        result,
        tokens_grad,
        owned[0],
        shared[0],
        output_owned,
        gate_up_owned,
        down_owned,
        shared[1],
        shared[2],
        shared[3],
        shared[4],
        shared[5],
        shared[6],
    )


def solution(mesh):
    placed = (
        P(("dp", "mp"), None),
        P("dp"),
        P("dp"),
        P("dp", "mp"),
        P("dp", None),
        P("mp", "dp"),
        P(None, "dp", "mp"),
        P("mp", "dp"),
        P("dp"),
        P("dp"),
        P("dp"),
        P("dp"),
        P("dp"),
        P("dp"),
        P(("dp", "mp"), None),
    )
    return jax.shard_map(
        local,
        mesh=mesh,
        in_specs=placed,
        out_specs=(
            P(("dp", "mp"), None),
            P(("dp", "mp"), None),
            P("dp", "mp"),
            P("dp", None),
            P("mp", "dp"),
            P(None, "dp", "mp"),
            P("mp", "dp"),
            P("dp"),
            P("dp"),
            P("dp"),
            P("dp"),
            P("dp"),
            P("dp"),
        ),
        check_vma=False,
    )
```

profile of v0, /device:TPU:0, one launch (start us, length us, event | category | flops | bytes accessed | tf_op | source)
XLA Modules:
  0.0 1172.3 jit_solution(1449548901311798915)
XLA Ops:
  15.7 39.0 %all-reduce.18 = (bf16[1152]{0:T(1024)(128)(2,1)S(1)}, bf16[256]{0:T(256)(128)(2,1)S(1)}, bf16[256]{0:T(256)(128)(2,1)S(1)}, bf16[1152]{0:T(1024)(128)(2,1)S(1)}...) all-reduce(bf16[1152]{0:T(1024)(128)(2,1)S(1)} %dynamic-update-slic, ...), channel_id=1, replica_groups=mesh['dp'=8,'mp'=4] {'dp'}, use_global_device_ids=true, to_apply=%add.4 | all-reduce | flops 5120 | bytes 20480
  60.9 31.9 %all_gather.58 = bf16[1152,256]{1,0:T(8,128)(2,1)S(1)} all-gather(bf16[144,256]{1,0:T(8,128)(2,1)} %param.26), channel_id=1, replica_groups=mesh['dp'=8,'mp'=4] {'dp'}, dimensions={0}, use_global_device_ids=true | all-gather | bytes 663552 | tf_op jit(solution)/shard_map/all_gather | solution.py:73
  101.5 33.6 %all_gather.62 = bf16[256,1152]{0,1:T(8,128)(2,1)S(1)} all-gather(bf16[256,144]{0,1:T(8,128)(2,1)S(1)} %copy-done.24), channel_id=1, replica_groups=mesh['dp'=8,'mp'=4] {'dp'}, dimensions={1}, use_global_device_ids=true | all-gather | bytes 663552 | tf_op jit(solution)/shard_map/all_gather | solution.py:75
  143.6 35.0 %reduce-scatter.9.cloned.1.call-done = f32[128,1152]{1,0:T(8,128)} async-done(((f32[512,1152]{1,0:T(8,128)}), f32[128,1152]{1,0:T(8,128)}) %reduce-scatter.9.cloned.1.call-update) | async-done | bytes 589840 | tf_op jit(solution)/shard_map/reduce_scatter | solution.py:148
  183.9 16.2 %all-gather.12.cloned.1.call-done = bf16[512,1152]{1,0:T(8,128)(2,1)} async-done(((bf16[128,1152]{1,0:T(8,128)(2,1)}), bf16[512,1152]{1,0:T(8,128)(2,1)}) %all-gather.12.cloned.1.call-update) | async-done | bytes 1179664 | tf_op jit(solution)/shard_map/all_gather | solution.py:156
  200.1 125.5 %all-gather.14.cloned.1.call-done = bf16[2,1152,1728]{2,1,0:T(8,128)(2,1)} async-done(((bf16[2,144,1728]{2,1,0:T(8,128)(2,1)}), bf16[2,1152,1728]{2,1,0:T(8,128)(2,1)}) %all-gather.14.cloned.1.call-update) | async-done | bytes 7962640 | tf_op jit(solution)/shard_map/all_gather | solution.py:76
  325.6 5.2 fusion.3
  332.6 4.9 multiply_convert_fusion.1
  337.6 61.1 %all-gather.16.cloned.1.call-done = bf16[1728,1152]{0,1:T(8,128)(2,1)} async-done(((bf16[1728,144]{0,1:T(8,128)(2,1)}), bf16[1728,1152]{0,1:T(8,128)(2,1)}) %all-gather.16.cloned.1.call-update) | async-done | bytes 3981328 | tf_op jit(solution)/shard_map/all_gather | solution.py:77
  398.7 6.5 convolution_convert_fusion.5
  405.2 24.1 %reduce-scatter.11.cloned.1.call-done = bf16[128,1152]{1,0:T(8,128)(2,1)} async-done(((bf16[512,1152]{1,0:T(8,128)(2,1)}), bf16[128,1152]{1,0:T(8,128)(2,1)}) %reduce-scatter.11.cloned.1.call-update) | async-done | bytes 294928 | tf_op jit(solution)/shard_map/reduce_scatter | solution.py:160
  434.6 17.2 %all-gather.18.cloned.1.call-done = bf16[512,1152]{1,0:T(8,128)(2,1)} async-done(((bf16[128,1152]{1,0:T(8,128)(2,1)}), bf16[512,1152]{1,0:T(8,128)(2,1)}) %all-gather.18.cloned.1.call-update) | async-done | bytes 1179664 | tf_op jit(solution)/shard_map/all_gather | solution.py:190
  451.8 9.6 multiply_convert_fusion
  461.4 6.0 fusion.2
  467.5 6.0 fusion.14
  473.5 25.8 %reduce-scatter.13.cloned.1.call-done = bf16[128,1152]{1,0:T(8,128)(2,1)} async-done(((bf16[512,1152]{1,0:T(8,128)(2,1)}), bf16[128,1152]{1,0:T(8,128)(2,1)}) %reduce-scatter.13.cloned.1.call-update) | async-done | bytes 294928 | tf_op jit(solution)/shard_map/reduce_scatter | solution.py:208
  507.1 16.9 %all-gather.20.cloned.1.call-done = bf16[512,1152]{1,0:T(8,128)(2,1)} async-done(((bf16[128,1152]{1,0:T(8,128)(2,1)}), bf16[512,1152]{1,0:T(8,128)(2,1)}) %all-gather.20.cloned.1.call-update) | async-done | bytes 1179664 | tf_op jit(solution)/shard_map/all_gather | solution.py:220
  532.1 10.7 collective-permute-done.3
  551.8 3.8 convolution_convert_fusion.4
  555.7 5.9 fusion.1
  561.7 4.4 fusion
  566.1 46.4 %reduce-scatter.19.cloned.1.call-done = bf16[144,512]{1,0:T(8,128)(2,1)} async-done(((bf16[1152,512]{1,0:T(8,128)(2,1)}), bf16[144,512]{1,0:T(8,128)(2,1)}) %reduce-scatter.19.cloned.1.call-update) | async-done | bytes 147472 | tf_op jit(solution)/shard_map/reduce_scatter | solution.py:289
  612.5 7.2 pad_maximum_fusion
  619.7 22.8 %copy.37 = bf16[1152,2,1728]{2,1,0:T(2,128)(2,1)} copy(bf16[1152,2,1728]{0,2,1:T(8,128)(2,1)} %pad_maximum_fusion) | data formatting | bytes 15925248 | tf_op jit(solution)/shard_map/stack | solution.py:201
  644.5 4.3 convolution_convert_fusion.2
  650.2 26.8 %reduce-scatter.21.cloned.1.call-done = bf16[144,256]{1,0:T(8,128)(2,1)} async-done(((bf16[1152,256]{1,0:T(8,128)(2,1)}), bf16[144,256]{1,0:T(8,128)(2,1)}) %reduce-scatter.21.cloned.1.call-update) | async-done | bytes 73744 | tf_op jit(solution)/shard_map/reduce_scatter | solution.py:292
  678.6 63.4 %reduce-scatter.17.cloned.1.call-done = bf16[144,256]{1,0:T(8,128)(2,1)} async-done(((bf16[1152,256]{1,0:T(8,128)(2,1)}), bf16[144,256]{1,0:T(8,128)(2,1)}) %reduce-scatter.17.cloned.1.call-update) | async-done | bytes 73744 | tf_op jit(solution)/shard_map/reduce_scatter | solution.py:286
  743.5 25.9 %reduce-scatter.15.cloned.1.call-done = bf16[128,1152]{1,0:T(8,128)(2,1)} async-done(((bf16[512,1152]{1,0:T(8,128)(2,1)}), bf16[128,1152]{1,0:T(8,128)(2,1)}) %reduce-scatter.15.cloned.1.call-update) | async-done | bytes 294928 | tf_op jit(solution)/shard_map/reduce_scatter | solution.py:275
  770.6 37.1 %all-reduce.17 = (bf16[1152]{0:T(1024)(128)(2,1)S(1)}, bf16[1152]{0:T(1024)(128)(2,1)S(1)}, bf16[1152]{0:T(1024)(128)(2,1)S(1)}, bf16[1152]{0:T(1024)(128)(2,1)S...) all-reduce(bf16[1152]{0:T(1024)(128)(2,1)S(1)} %get-tuple-element.9, ...), channel_id=11, replica_groups=mesh['dp'=8,'mp'=4] {'dp'}, use_global_device_ids=true, to_apply=%region_26.27.clone | all-reduce | flops 5120 | bytes 20480
  808.2 5.9 all-reduce.19
  821.1 252.3 %all-reduce.25.cloned.1.call-done = bf16[1152,2,1728]{2,1,0:T(2,128)(2,1)} async-done(((bf16[1152,2,1728]{2,1,0:T(2,128)(2,1)}), bf16[1152,2,1728]{2,1,0:T(2,128)(2,1)}) %all-reduce.25.cloned.1.call-update) | async-done | bytes 7962640
  1076.8 86.8 %reduce-scatter.23.cloned.1.call-done = bf16[144,1728]{1,0:T(8,128)(2,1)} async-done(((bf16[1152,1728]{1,0:T(8,128)(2,1)}), bf16[144,1728]{1,0:T(8,128)(2,1)}) %reduce-scatter.23.cloned.1.call-update) | async-done | bytes 497680 | tf_op jit(solution)/shard_map/reduce_scatter | solution.py:298
  (280 shorter events, 86.1 us)
Async XLA Ops:
  7.2 85.7 %all-gather.10.cloned.1.call-start = ((), (), s32[]{:S(2)}) async-start(), calls=%async_computation.9 | async-start | bytes 1327104 | tf_op jit(solution)/shard_map/all_gather | solution.py:74
  7.9 86.4 %all-gather.8.cloned.1.call-start = ((), (), s32[]{:S(2)}) async-start(), calls=%async_computation.8 | async-start | bytes 1474560 | tf_op jit(solution)/shard_map/all_gather | solution.py:108
  58.2 120.4 %reduce-scatter.9.cloned.1.call-start = ((), (), s32[]{:S(2)}) async-start(), calls=%async_computation.10 | async-start | bytes 2949120 | tf_op jit(solution)/shard_map/reduce_scatter | solution.py:148
  58.9 76.2 %collective-permute-start = (bf16[512]{0:T(512)(128)(2,1)S(1)}, bf16[512]{0:T(512)(128)(2,1)S(1)}, u32[]{:S(2)}, u32[]{:S(2)}) collective-permute-start(bf16[512]{0:T(512)(128)(2,1)S(1)} %add_convert_fusion), channel_id=1, source_target_pairs={{0,4},{4,8},{8,12},{12,16},{16,20},{20,24},{24,28},{1,5},{5,9},{9,... | collective-permute-start | bytes 3080 | tf_op jit(solution)/shard_map/ppermute | solution.py:18
  100.2 36.7 %collective-permute-start.1 = (bf16[512,256]{1,0:T(8,128)(2,1)S(1)}, bf16[512,256]{1,0:T(8,128)(2,1)S(1)}, u32[]{:S(2)}, u32[]{:S(2)}) collective-permute-start(bf16[512,256]{1,0:T(8,128)(2,1)S(1)} %pad_maximum_fusion.8), channel_id=1, source_target_pairs={{0,4},{4,8},{8,12},{12,16},{16,20},{20,24},{24,28},{1,5},{5,9},{9,... | collective-permute-start | bytes 786440 | tf_op jit(solution)/shard_map/ppermute | solution.py:18
  135.2 5.6 collective-permute-start.2
  143.5 56.6 %all-gather.12.cloned.1.call-start = ((), (), s32[]{:S(2)}) async-start(), calls=%async_computation.11 | async-start | bytes 1474560 | tf_op jit(solution)/shard_map/all_gather | solution.py:156
  181.6 149.3 %copy-start.52 = (f32[128]{0:T(128)}, f32[128]{0:T(128)S(1)}, u32[]{:S(2)}) copy-start(f32[128]{0:T(128)S(1)} %get-tuple-element.114) | copy-start | bytes 1540
  181.6 149.3 %copy-start.48 = (f32[128]{0:T(128)}, f32[128]{0:T(128)S(1)}, u32[]{:S(2)}) copy-start(f32[128]{0:T(128)S(1)} %fusion.80) | copy-start | bytes 1540
  182.5 143.2 %all-gather.14.cloned.1.call-start = ((), (), s32[]{:S(2)}) async-start(), calls=%async_computation.12 | async-start | bytes 9289728 | tf_op jit(solution)/shard_map/all_gather | solution.py:76
  183.1 215.6 %all-gather.16.cloned.1.call-start = ((), (), s32[]{:S(2)}) async-start(), calls=%async_computation.13 | async-start | bytes 4644864 | tf_op jit(solution)/shard_map/all_gather | solution.py:77
  183.7 245.7 %reduce-scatter.11.cloned.1.call-start = ((), (), s32[]{:S(2)}) async-start(), calls=%async_computation.14 | async-start | bytes 1474560 | tf_op jit(solution)/shard_map/reduce_scatter | solution.py:160
  405.2 46.6 %all-gather.18.cloned.1.call-start = ((), (), s32[]{:S(2)}) async-start(), calls=%async_computation.15 | async-start | bytes 1474560 | tf_op jit(solution)/shard_map/all_gather | solution.py:190
  405.2 56.1 %copy-start.19 = (f32[1152]{0:T(1024)}, f32[1152]{0:T(1024)S(1)}, u32[]{:S(2)}) copy-start(f32[1152]{0:T(1024)S(1)} %convert_element_type.188) | copy-start | bytes 13828
  434.2 65.1 %reduce-scatter.13.cloned.1.call-start = ((), (), s32[]{:S(2)}) async-start(), calls=%async_computation.16 | async-start | bytes 1474560 | tf_op jit(solution)/shard_map/reduce_scatter | solution.py:208
  473.4 50.6 %all-gather.20.cloned.1.call-start = ((), (), s32[]{:S(2)}) async-start(), calls=%async_computation.17 | async-start | bytes 1474560 | tf_op jit(solution)/shard_map/all_gather | solution.py:220
  506.4 106.0 %reduce-scatter.19.cloned.1.call-start = ((), (), s32[]{:S(2)}) async-start(), calls=%async_computation.20 | async-start | bytes 1327104 | tf_op jit(solution)/shard_map/reduce_scatter | solution.py:289
  526.6 18.3 %collective-permute-start.4 = (bf16[512,256]{1,0:T(8,128)(2,1)S(1)}, bf16[512,256]{1,0:T(8,128)(2,1)S(1)}, u32[]{:S(2)}, u32[]{:S(2)}) collective-permute-start(bf16[512,256]{1,0:T(8,128)(2,1)S(1)} %slice.147), channel_id=1, source_target_pairs={{4,0},{8,4},{12,8},{16,12},{20,16},{24,20},{28,24},{5,1},{9,5},{13... | collective-permute-start | bytes 786440 | tf_op jit(solution)/shard_map/ppermute | solution.py:18
  530.3 12.5 %collective-permute-start.3 = (bf16[512,256]{1,0:T(8,128)(2,1)S(1)}, bf16[512,256]{1,0:T(8,128)(2,1)S(1)}, u32[]{:S(2)}, u32[]{:S(2)}) collective-permute-start(bf16[512,256]{1,0:T(8,128)(2,1)S(1)} %slice.148), channel_id=1, source_target_pairs={{4,0},{8,4},{12,8},{16,12},{20,16},{24,20},{28,24},{5,1},{9,5},{13... | collective-permute-start | bytes 786440 | tf_op jit(solution)/shard_map/ppermute | solution.py:18
  548.1 128.9 %reduce-scatter.21.cloned.1.call-start = ((), (), s32[]{:S(2)}) async-start(), calls=%async_computation.22 | async-start | bytes 663552 | tf_op jit(solution)/shard_map/reduce_scatter | solution.py:292
  550.9 191.1 %reduce-scatter.17.cloned.1.call-start = ((), (), s32[]{:S(2)}) async-start(), calls=%async_computation.19 | async-start | bytes 663552 | tf_op jit(solution)/shard_map/reduce_scatter | solution.py:286
  551.8 217.6 %reduce-scatter.15.cloned.1.call-start = ((), (), s32[]{:S(2)}) async-start(), calls=%async_computation.18 | async-start | bytes 1474560 | tf_op jit(solution)/shard_map/reduce_scatter | solution.py:275
  555.7 263.7 %all-reduce.23.cloned.1.call-start = ((), (), s32[]{:S(2)}) async-start(), calls=%async_computation.21 | async-start | bytes 294912 | tf_op jit(solution)/shard_map/psum | solution.py:324
  612.4 460.9 %all-reduce.25.cloned.1.call-start = ((), (), s32[]{:S(2)}) async-start(), calls=%async_computation.24 | async-start | bytes 16515072
  642.6 520.9 %reduce-scatter.23.cloned.1.call-start = ((), (), s32[]{:S(2)}) async-start(), calls=%async_computation.23 | async-start | bytes 4644864 | tf_op jit(solution)/shard_map/reduce_scatter | solution.py:298
  648.7 120.7 %copy-start.4 = (bf16[128,1152]{1,0:T(8,128)(2,1)S(1)}, bf16[128,1152]{1,0:T(8,128)(2,1)}, u32[]{:S(2)}) copy-start(bf16[128,1152]{1,0:T(8,128)(2,1)} %param.23) | copy-start | bytes 884740
  648.7 120.7 %copy-start.47 = (f32[128]{0:T(128)S(1)}, f32[128]{0:T(128)}, u32[]{:S(2)}) copy-start(f32[128]{0:T(128)} %copy-done.46) | copy-start | bytes 1540
  648.7 121.9 %copy-start.35 = (bf16[1152]{0:T(1024)(128)(2,1)S(1)}, bf16[1152]{0:T(1024)(128)(2,1)}, u32[]{:S(2)}) copy-start(bf16[1152]{0:T(1024)(128)(2,1)} %get-tuple-element.91) | copy-start | bytes 6916
  648.7 121.9 %copy-start.36 = (bf16[1152]{0:T(1024)(128)(2,1)S(1)}, bf16[1152]{0:T(1024)(128)(2,1)}, u32[]{:S(2)}) copy-start(bf16[1152]{0:T(1024)(128)(2,1)} %get-tuple-element.89) | copy-start | bytes 6916
  648.7 121.9 %copy-start.37 = (bf16[1152]{0:T(1024)(128)(2,1)S(1)}, bf16[1152]{0:T(1024)(128)(2,1)}, u32[]{:S(2)}) copy-start(bf16[1152]{0:T(1024)(128)(2,1)} %get-tuple-element.87) | copy-start | bytes 6916
  648.7 168.7 %copy-start.54 = (f32[128]{0:T(128)S(1)}, f32[128]{0:T(128)}, u32[]{:S(2)}) copy-start(f32[128]{0:T(128)} %copy-done.53) | copy-start | bytes 1540
  648.8 168.7 %copy-start.6 = (f32[128,1152]{1,0:T(8,128)S(1)}, f32[128,1152]{1,0:T(8,128)}, u32[]{:S(2)}) copy-start(f32[128,1152]{1,0:T(8,128)} %copy-done.5) | copy-start | bytes 1769476
  (59 other events, 733.7 us)
Sparse Core Ops, SparseCore 0:
  10.2 43.8 all-gather.9
  58.3 14.6 all-gather.7
  143.6 34.8 reduce-scatter.8
  182.6 17.4 all-gather.11
  202.4 123.2 all-gather.13
  327.9 70.7 all-gather.15
  405.3 23.9 reduce-scatter.10
  434.3 17.4 all-gather.17
  473.6 25.7 reduce-scatter.12
  506.6 17.4 all-gather.19
  548.3 64.1 reduce-scatter.18
  615.9 61.0 reduce-scatter.20
  680.9 61.0 reduce-scatter.16
  744.6 24.7 reduce-scatter.14
  771.6 30.7 all-reduce.22
  806.5 266.8 all-reduce.24
  1076.8 86.6 reduce-scatter.22
where the time goes:
time: 1180 us; the launch traced here: 1170 us
  waiting for transfers between devices  838 us (71%)
  blocking collectives  148 us (13%)
  matrix products  71 us (6%)
  other arithmetic  46.7 us (4%)
  local copies, waits for them, and re-layouts  42.2 us (4%)
  between operations  17.9 us (2%)
    unnamed x18, waiting for transfers between devices  254 us
    all_gather x1, waiting for transfers between devices, local(): lax.all_gather(gate_up_weight, 'dp', axis=1, tiled=True)  126 us
    reduce_scatter x1, waiting for transfers between devices, local(): lax.psum_scatter(down_grad_turned.astype(jnp.bfloat16), 'dp', scatter_dim...  86.8 us
    unnamed x2, blocking collectives  76.1 us
    reduce_scatter x1, waiting for transfers between devices, local(): lax.psum_scatter(joint_grad[:, :head_size].astype(jnp.bfloat16), 'dp', sc...  63.4 us
    all_gather x1, waiting for transfers between devices, local(): lax.all_gather(down_weight, 'dp', axis=1, tiled=True)  61.1 us
    reduce_scatter x1, waiting for transfers between devices, local(): lax.psum_scatter(joint_grad[:, head_size:].astype(jnp.bfloat16), 'dp', sc...  46.4 us
    reduce_scatter x1, waiting for transfers between devices, local(): lax.psum_scatter(jnp.dot(attended, output_full, preferred_element_type=jn...  35 us
  transfers between devices with their start and end apart: 22, of which 16 were waited for; matrix products, arithmetic and copies ran while one was open for 9% of the time, Pallas kernels for 0%

commit v1 on v0

v1 whole, which is shorter than its diff:
```python
from functools import partial

import jax
import jax.numpy as jnp
from jax import lax
from jax.sharding import PartitionSpec as P

WINDOW = 512


EPS = 1e-06
NEG = -1e30


def from_behind(value, axis, steps):
    count = lax.axis_size(axis)
    leading, last = (max(0, -steps), min(count, count - steps))
    return lax.ppermute(value, axis, [(source, source + steps) for source in range(leading, last)])


def shifted(value, axis, shift):
    count = lax.axis_size(axis)
    return lax.ppermute(value, axis, [(i, (i + shift) % count) for i in range(count)])


def gather_relative(value):
    count = lax.axis_size("mp")
    return [value] + [shifted(value, "mp", -step) for step in range(1, count)]


def gather_ordered(value):
    count = lax.axis_size("mp")
    rows = value.shape[0]
    me = lax.axis_index("mp")
    whole = jnp.zeros((count * rows,) + value.shape[1:], value.dtype)
    for step, block in enumerate(gather_relative(value)):
        owner = lax.rem(me + step, count)
        whole = lax.dynamic_update_slice_in_dim(whole, block, owner * rows, axis=0)
    return whole


def scatter_relative(blocks):
    total = blocks[0].astype(jnp.float32)
    for step in range(1, len(blocks)):
        total = total + shifted(blocks[step], "mp", step).astype(jnp.float32)
    return total


def scatter_ordered(value):
    count = lax.axis_size("mp")
    rows = value.shape[0] // count
    me = lax.axis_index("mp")
    return scatter_relative(
        [
            lax.dynamic_slice_in_dim(value, lax.rem(me + step, count) * rows, rows, axis=0)
            for step in range(count)
        ]
    )


def split_rows(value):
    rows = value.shape[0] // lax.axis_size("mp")
    return [value[i * rows : (i + 1) * rows] for i in range(lax.axis_size("mp"))]


def sum_over_mp(value):
    total = value.astype(jnp.float32)
    for step in range(1, lax.axis_size("mp")):
        total = total + shifted(value, "mp", step).astype(jnp.float32)
    return total


def normalize(value, gain):
    return value * lax.rsqrt(jnp.mean(value * value, axis=-1, keepdims=True) + EPS) * gain


def rotary_tables(positions, width):
    half_width = width // 2
    frequency = jnp.power(10000.0, -jnp.arange(half_width, dtype=jnp.float32) * (2.0 / width))
    angles = positions.astype(jnp.float32)[:, None] * frequency[None, :]
    return (jnp.cos(angles), jnp.sin(angles))


def rotate(value, cosine, sine):
    half_width = value.shape[-1] // 2
    first_half = value[..., :half_width]
    second_half = value[..., half_width:]
    return jnp.concatenate(
        [first_half * cosine - second_half * sine, second_half * cosine + first_half * sine],
        axis=-1,
    )


def prepare_head(pre_value, gain, cosine, sine):
    return rotate(normalize(pre_value, gain), cosine, sine)


def gated_units(gate, up_part):
    return jax.nn.gelu(gate, approximate=True) * up_part


def norm_back(value, gain, grad):
    unused, pull = jax.vjp(normalize, value, gain)
    return pull(grad)


def local(
    tokens,
    segment_ids,
    positions,
    q_weight,
    kv_weight,
    o_weight,
    gate_up_weight,
    down_weight,
    attn_pre_gain,
    attn_post_gain,
    ff_pre_gain,
    ff_post_gain,
    query_gain,
    key_gain,
    out_grad,
):
    rows = q_weight.shape[0]
    head_size = q_weight.shape[1]
    width = rows * lax.axis_size("dp")
    gain_rows = query_gain.shape[0]
    small_gains = [
        jnp.pad(item, (0, rows - gain_rows)) for item in (query_gain, key_gain)
    ]
    gain_columns = jnp.stack(
        [attn_pre_gain, attn_post_gain, ff_pre_gain, ff_post_gain] + small_gains, axis=1
    )
    gain_columns = jnp.pad(gain_columns, ((0, 0), (0, 128 - gain_columns.shape[1])))
    packed = jnp.concatenate(
        [q_weight, kv_weight, jnp.transpose(o_weight), gain_columns], axis=1
    )
    packed_full = lax.all_gather(packed, "dp", axis=0, tiled=True)
    gate_up_full = lax.all_gather(gate_up_weight, "dp", axis=1, tiled=True)
    down_full = lax.all_gather(down_weight, "dp", axis=1, tiled=True)
    joint_weight = packed_full[:, : 3 * head_size]
    output_turned = packed_full[:, 3 * head_size : 4 * head_size]
    gain_block = jnp.transpose(packed_full[:, 4 * head_size :]).astype(jnp.float32)
    gains = [gain_block[i] for i in range(4)] + [
        gain_block[i].reshape(-1, rows)[:, :gain_rows].reshape(-1) for i in (4, 5)
    ]
    length = segment_ids.shape[0]
    reach = -(-WINDOW // length)
    block_size = min(512, length)
    score_scale = head_size ** (-0.5)
    span = block_size + WINDOW
    cosine, sine = rotary_tables(positions, head_size)
    distance = (
        jnp.arange(block_size, dtype=jnp.int32)[:, None]
        + WINDOW
        - jnp.arange(span, dtype=jnp.int32)[None, :]
    )
    inside = (distance >= 0) & (distance < WINDOW)
    residual = tokens.astype(jnp.float32)
    attn_local = normalize(residual, gains[0]).astype(jnp.bfloat16)
    attn_in = gather_ordered(attn_local)
    projected = jnp.dot(attn_in, joint_weight, preferred_element_type=jnp.float32)
    query_pre = projected[:, :head_size]
    key_pre = projected[:, head_size : 2 * head_size]
    value_pre = projected[:, 2 * head_size :]
    queries = prepare_head(query_pre, gains[4], cosine, sine).astype(jnp.bfloat16)
    keys = prepare_head(key_pre, gains[5], cosine, sine).astype(jnp.bfloat16)
    values = value_pre.astype(jnp.bfloat16)
    marks = (segment_ids + 1).astype(jnp.bfloat16)
    key_parts, value_parts, mark_parts = ([], [], [])
    step = 1
    moved = from_behind((keys, values, marks), "dp", step)
    key_parts.append(moved[0])
    value_parts.append(moved[1])
    mark_parts.append(moved[2])
    all_keys = jnp.concatenate(key_parts + [keys], axis=0)
    all_values = jnp.concatenate(value_parts + [values], axis=0)
    all_marks = jnp.concatenate(mark_parts + [marks], axis=0)

    def block_parts(start):
        first_key = start + reach * length - WINDOW
        visible = inside & (marks[:, None] == all_marks[None, :])
        product = (
            jnp.einsum("qd,kd->qk", queries, all_keys, preferred_element_type=jnp.float32)
            * score_scale
        )
        return (first_key, queries, all_keys, all_values, jnp.where(visible, product, NEG))

    mixed_parts, total_parts = ([], [])
    start = 0
    first_key, query_block, key_block, value_block, scores = block_parts(start)
    highest = jnp.max(scores, axis=-1, keepdims=True)
    expo = jnp.exp(scores - highest)
    denominator = jnp.sum(expo, axis=-1, keepdims=True)
    probs = (expo / denominator).astype(jnp.bfloat16)
    mixed_parts.append(jnp.dot(probs, value_block, preferred_element_type=jnp.float32))
    total_parts.append(highest + jnp.log(denominator))
    attended = mixed_parts[0].astype(jnp.bfloat16)
    log_totals = total_parts[0]
    attn_out = scatter_ordered(
        jnp.einsum(
            "le,de->ld", attended, output_turned, preferred_element_type=jnp.float32
        ).astype(jnp.bfloat16)
    )
    middle = residual + normalize(attn_out, gains[1])
    ff_local = normalize(middle, gains[2]).astype(jnp.bfloat16)
    ff_in = jnp.concatenate(gather_relative(ff_local), axis=0)
    gate = jnp.dot(ff_in, gate_up_full[0], preferred_element_type=jnp.float32)
    up_part = jnp.dot(ff_in, gate_up_full[1], preferred_element_type=jnp.float32)
    hidden = gated_units(gate, up_part).astype(jnp.bfloat16)
    ff_out = scatter_relative(
        split_rows(
            jnp.dot(hidden, down_full, preferred_element_type=jnp.float32).astype(jnp.bfloat16)
        )
    )
    result = (middle + normalize(ff_out, gains[3])).astype(jnp.bfloat16)
    top_grad = out_grad.astype(jnp.float32)
    ff_out_grad, ff_post_grad = norm_back(ff_out, gains[3], top_grad)
    ff_grad_all = jnp.concatenate(gather_relative(ff_out_grad.astype(jnp.bfloat16)), axis=0)
    hidden_grad = jnp.einsum(
        "ld,fd->lf", ff_grad_all, down_full, preferred_element_type=jnp.float32
    )
    down_grad_turned = jnp.einsum(
        "ld,lf->df", ff_grad_all, hidden, preferred_element_type=jnp.float32
    )
    unused, unit_pull = jax.vjp(gated_units, gate, up_part)
    gate_grad, up_grad = unit_pull(hidden_grad)
    gate_low = gate_grad.astype(jnp.bfloat16)
    up_low = up_grad.astype(jnp.bfloat16)
    gate_turned = jnp.einsum("ld,lf->df", ff_in, gate_low, preferred_element_type=jnp.float32)
    up_turned = jnp.einsum("ld,lf->df", ff_in, up_low, preferred_element_type=jnp.float32)
    ff_in_partial = (
        jnp.einsum("lf,df->ld", gate_low, gate_up_full[0], preferred_element_type=jnp.float32)
        + jnp.einsum("lf,df->ld", up_low, gate_up_full[1], preferred_element_type=jnp.float32)
    ).astype(jnp.bfloat16)
    ff_in_partial, down_low, gate_turned_low, up_turned_low = lax.optimization_barrier(
        (
            ff_in_partial,
            down_grad_turned.astype(jnp.bfloat16),
            gate_turned.astype(jnp.bfloat16),
            up_turned.astype(jnp.bfloat16),
        )
    )
    feed_forward_owned = tuple(
        lax.psum_scatter(item, "dp", scatter_dimension=0, tiled=True)
        for item in (down_low, gate_turned_low, up_turned_low)
    )
    ff_in_grad = scatter_relative(split_rows(ff_in_partial))
    middle_part, ff_pre_grad = norm_back(middle, gains[2], ff_in_grad)
    middle_grad = top_grad + middle_part
    attn_out_grad, attn_post_grad = norm_back(attn_out, gains[1], middle_grad)
    attn_grad_all = gather_ordered(attn_out_grad.astype(jnp.bfloat16))
    attended_grad = jnp.einsum(
        "ld,de->le", attn_grad_all, output_turned, preferred_element_type=jnp.float32
    ).astype(jnp.bfloat16)
    output_grad_turned = jnp.einsum(
        "ld,le->de", attn_grad_all, attended, preferred_element_type=jnp.float32
    )
    key_grad_all = jnp.zeros(((reach + 1) * length, head_size), jnp.float32)
    value_grad_all = jnp.zeros(((reach + 1) * length, head_size), jnp.float32)
    start = 0
    first_key, query_block, key_block, value_block, scores = block_parts(start)
    probs = jnp.exp(scores - log_totals)
    probs_low = probs.astype(jnp.bfloat16)
    value_grad_all = value_grad_all.at[first_key : first_key + span].add(
        jnp.einsum("qk,qd->kd", probs_low, attended_grad, preferred_element_type=jnp.float32)
    )
    prob_grad = jnp.einsum(
        "qd,kd->qk", attended_grad, value_block, preferred_element_type=jnp.float32
    )
    inner = jnp.sum(probs * prob_grad, axis=-1, keepdims=True)
    score_grad = (probs * (prob_grad - inner)).astype(jnp.bfloat16)
    query_parts = jnp.dot(score_grad, key_block, preferred_element_type=jnp.float32) * score_scale
    key_grad_all = key_grad_all.at[first_key : first_key + span].add(
        jnp.einsum("qk,qd->kd", score_grad, query_block, preferred_element_type=jnp.float32)
        * score_scale
    )
    own_keys = key_grad_all[reach * length :]
    own_values = value_grad_all[reach * length :]
    step = 1
    slot = reach - step
    returned = (
        from_behind(
            key_grad_all[slot * length : (slot + 1) * length].astype(jnp.bfloat16), "dp", -step
        ).astype(jnp.float32),
        from_behind(
            value_grad_all[slot * length : (slot + 1) * length].astype(jnp.bfloat16), "dp", -step
        ).astype(jnp.float32),
    )
    own_keys = own_keys + returned[0]
    own_values = own_values + returned[1]
    unused, query_pull = jax.vjp(
        partial(prepare_head, cosine=cosine, sine=sine), query_pre, gains[4]
    )
    query_pre_grad, query_gain_grad = query_pull(query_parts)
    unused, key_pull = jax.vjp(
        partial(prepare_head, cosine=cosine, sine=sine), key_pre, gains[5]
    )
    key_pre_grad, key_gain_grad = key_pull(own_keys)
    joint_grad_rows = jnp.concatenate([query_pre_grad, key_pre_grad, own_values], axis=1).astype(
        jnp.bfloat16
    )
    joint_grad = jnp.einsum(
        "ld,lc->dc", attn_in, joint_grad_rows, preferred_element_type=jnp.float32
    )
    attn_in_grad = scatter_ordered(
        jnp.einsum(
            "lc,dc->ld", joint_grad_rows, joint_weight, preferred_element_type=jnp.float32
        ).astype(jnp.bfloat16)
    )
    tokens_part, attn_pre_grad = norm_back(residual, gains[0], attn_in_grad)
    tokens_grad = middle_grad + tokens_part
    small_grads = [
        jnp.pad(item.reshape(-1, gain_rows), ((0, 0), (0, rows - gain_rows))).reshape(-1)
        for item in (query_gain_grad, key_gain_grad)
    ]
    gain_grads = jnp.stack(
        [attn_pre_grad, attn_post_grad, ff_pre_grad, ff_post_grad] + small_grads, axis=1
    )
    gain_grads = jnp.pad(gain_grads, ((0, 0), (0, 128 - gain_grads.shape[1])))
    packed_grad = jnp.concatenate(
        [
            joint_grad[:, :head_size].astype(jnp.bfloat16),
            output_grad_turned.astype(jnp.bfloat16),
            joint_grad[:, head_size:].astype(jnp.bfloat16),
            gain_grads.astype(jnp.bfloat16),
        ],
        axis=1,
    )
    packed_grad, feed_forward_owned = lax.optimization_barrier(
        (packed_grad, feed_forward_owned)
    )
    down_owned = jnp.transpose(feed_forward_owned[0]).astype(jnp.float32)
    gate_up_owned = jnp.stack(feed_forward_owned[1:], axis=0).astype(jnp.float32)
    packed_owned = lax.psum_scatter(packed_grad, "dp", scatter_dimension=0, tiled=True)
    query_owned = packed_owned[:, :head_size].astype(jnp.float32)
    output_owned = jnp.transpose(packed_owned[:, head_size : 2 * head_size]).astype(jnp.float32)
    summed = sum_over_mp(packed_owned[:, 2 * head_size :])
    keyval_owned = summed[:, : 2 * head_size]
    gain_owned = jnp.transpose(summed[:, 2 * head_size :])
    return (
        result,
        tokens_grad,
        query_owned,
        keyval_owned,
        output_owned,
        gate_up_owned,
        down_owned,
        gain_owned[0],
        gain_owned[1],
        gain_owned[2],
        gain_owned[3],
        gain_owned[4, :gain_rows],
        gain_owned[5, :gain_rows],
    )


def solution(mesh):
    placed = (
        P(("dp", "mp"), None),
        P("dp"),
        P("dp"),
        P("dp", "mp"),
        P("dp", None),
        P("mp", "dp"),
        P(None, "dp", "mp"),
        P("mp", "dp"),
        P("dp"),
        P("dp"),
        P("dp"),
        P("dp"),
        P("dp"),
        P("dp"),
        P(("dp", "mp"), None),
    )
    return jax.shard_map(
        local,
        mesh=mesh,
        in_specs=placed,
        out_specs=(
            P(("dp", "mp"), None),
            P(("dp", "mp"), None),
            P("dp", "mp"),
            P("dp", None),
            P("mp", "dp"),
            P(None, "dp", "mp"),
            P("mp", "dp"),
            P("dp"),
            P("dp"),
            P("dp"),
            P("dp"),
            P("dp"),
            P("dp"),
        ),
        check_vma=False,
    )
```

time: 1180 us -> 740 us (0.63)
  waiting for transfers between devices: 838 us -> 522 us
  blocking collectives: 148 us -> 0 us
  starting transfers between devices: 8.59 us -> 46.7 us
  other arithmetic: 46.7 us -> 22.5 us
  local copies, waits for them, and re-layouts: 42.2 us -> 65.8 us
    reduce_scatter x8 -> x0, waiting for transfers between devices: 334 us -> none  [the longest x1 86.8 us: local(): lax.psum_scatter(down_grad_turned.astype(jnp.bfloat16), 'dp', scatter_dim...]
    ppermute x0 -> x27, waiting for transfers between devices: none -> 91.2 us  [shifted(): lax.ppermute(value, axis, [(i, (i + shift) % count) for i in range(count)])]
    unnamed x2 -> x0, blocking collectives: 76.1 us -> none
    all_gather x7 -> x3, waiting for transfers between devices: 237 us -> 168 us  [the longest x1 59.2 us: local(): down_full = lax.all_gather(down_weight, 'dp', axis=1, tiled=True)]
    all_gather x2 -> x0, blocking collectives: 65.5 us -> none  [the longest x1 33.6 us: local(): lax.all_gather(o_weight, 'dp', axis=1, tiled=True)]
    ppermute x0 -> x27, starting transfers between devices: none -> 27 us  [shifted(): lax.ppermute(value, axis, [(i, (i + shift) % count) for i in range(count)])]
    unnamed x159 -> x175, local copies, waits for them, and re-layouts: 15.9 us -> 35.3 us
    another operation x1 -> x18, local copies, waits for them, and re-layouts: 22.8 us -> 8.39 us  [the longest x7 5.34 us: local(): jnp.stack([attn_pre_grad, attn_post_grad, ff_pre_grad, ff_post_grad] + sm...]
  transfers between devices with their start and end apart: 22 -> 39, of which waited for: 16 -> 32; matrix products, arithmetic and copies ran while one was open for 9% -> 11% of each run, Pallas kernels for 0% -> 0%
where the time goes in v1:
time: 740 us; the launch traced here: 732 us
  waiting for transfers between devices  522 us (71%)
  local copies, waits for them, and re-layouts  65.8 us (9%)
  matrix products  59.8 us (8%)
  starting transfers between devices  46.7 us (6%)
  other arithmetic  22.5 us (3%)
  between operations  15.8 us (2%)
    unnamed x11, waiting for transfers between devices  246 us
    ppermute x27, waiting for transfers between devices, shifted(): lax.ppermute(value, axis, [(i, (i + shift) % count) for i in range(count)])  91.2 us
    all_gather x1, waiting for transfers between devices, local(): down_full = lax.all_gather(down_weight, 'dp', axis=1, tiled=True)  59.2 us
    all_gather x1, waiting for transfers between devices, local(): packed_full = lax.all_gather(packed, 'dp', axis=0, tiled=True)  56.9 us
    all_gather x1, waiting for transfers between devices, local(): gate_up_full = lax.all_gather(gate_up_weight, 'dp', axis=1, tiled=True)  51.6 us
    unnamed x175, local copies, waits for them, and re-layouts  35.3 us
    ppermute x27, starting transfers between devices, shifted(): lax.ppermute(value, axis, [(i, (i + shift) % count) for i in range(count)])  27 us
    ppermute x5, starting transfers between devices, from_behind(): lax.ppermute(value, axis, [(source, source + steps) for source in range(l...  19.4 us
  transfers between devices with their start and end apart: 39, of which 32 were waited for; matrix products, arithmetic and copies ran while one was open for 11% of the time, Pallas kernels for 0%

profile of v1, /device:TPU:0, one launch (start us, length us, event | category | flops | bytes accessed | tf_op | source)
XLA Modules:
  0.0 732.3 jit_solution(13621012869615528322)
XLA Ops:
  14.2 56.9 %all-gather.4.cloned.1.call-done = bf16[1152,1152]{1,0:T(8,128)(2,1)} async-done(((bf16[144,1152]{1,0:T(8,128)(2,1)}), bf16[1152,1152]{1,0:T(8,128)(2,1)}) %all-gather.4.cloned.1.call-update) | async-done | bytes 2654224 | tf_op jit(solution)/shard_map/all_gather | solution.py:138
  76.5 3.9 collective-permute-done.1
  80.4 9.1 %collective-permute-done.2 = bf16[128,1152]{1,0:T(8,128)(2,1)S(1)} collective-permute-done((bf16[128,1152]{1,0:T(8,128)(2,1)S(1)}, bf16[128,1152]{1,0:T(8,128)(2,1)S(1)}, u32[]{:S(2)}, u32[]{:S(2)}) %collective-permute-start.2) | collective-permute-done | bytes 294944 | tf_op jit(solution)/shard_map/ppermute | solution.py:23
  97.4 4.3 collective-permute-start
  103.1 10.1 %collective-permute-start.5 = (bf16[512,256]{1,0:T(8,128)(2,1)S(1)}, bf16[512,256]{1,0:T(8,128)(2,1)S(1)}, u32[]{:S(2)}, u32[]{:S(2)}) collective-permute-start(bf16[512,256]{1,0:T(8,128)(2,1)S(1)} %slice.321), channel_id=1, source_target_pairs={{0,4},{4,8},{8,12},{12,16},{16,20},{20,24},{24,28},{1,5},{5,9},{9,... | collective-permute-start | bytes 786440 | tf_op jit(solution)/shard_map/ppermute | solution.py:18
  120.8 5.8 collective-permute-done.8
  126.5 7.6 %collective-permute-done.7 = bf16[128,1152]{1,0:T(8,128)(2,1)S(1)} collective-permute-done((bf16[128,1152]{1,0:T(8,128)(2,1)S(1)}, bf16[128,1152]{1,0:T(8,128)(2,1)S(1)}, u32[]{:S(2)}, u32[]{:S(2)}) %collective-permute-start.7) | collective-permute-done | bytes 294944 | tf_op jit(solution)/shard_map/ppermute | solution.py:23
  136.7 11.9 %collective-permute-start.9 = (bf16[128,1152]{1,0:T(8,128)(2,1)S(1)}, bf16[128,1152]{1,0:T(8,128)(2,1)}, u32[]{:S(2)}, u32[]{:S(2)}) collective-permute-start(bf16[128,1152]{1,0:T(8,128)(2,1)S(1)} %multiply_convert_fusion.3), channel_id=1, source_target_pairs={{0,3},{1,0},{2,1},{3,2},{4,7},{5,4},{6,5},{7,6},{8,11},{9,8},{10,9... | collective-permute-start | bytes 884744 | tf_op jit(solution)/shard_map/ppermute | solution.py:23
  152.8 51.6 %all-gather.6.cloned.1.call-done = bf16[2,1152,1728]{2,1,0:T(8,128)(2,1)} async-done(((bf16[2,144,1728]{2,1,0:T(8,128)(2,1)}), bf16[2,1152,1728]{2,1,0:T(8,128)(2,1)}) %all-gather.6.cloned.1.call-update) | async-done | bytes 7962640 | tf_op jit(solution)/shard_map/all_gather | solution.py:139
  204.4 5.2 fusion.2
  211.4 6.8 multiply_convert_fusion.1
  218.2 59.2 %all-gather.8.cloned.1.call-done = bf16[1728,1152]{0,1:T(8,128)(2,1)} async-done(((bf16[1728,144]{0,1:T(8,128)(2,1)}), bf16[1728,1152]{0,1:T(8,128)(2,1)}) %all-gather.8.cloned.1.call-update) | async-done | bytes 3981328 | tf_op jit(solution)/shard_map/all_gather | solution.py:140
  277.4 5.3 convolution_convert_fusion.5
  284.6 4.7 collective-permute-done.14
  289.2 9.2 %collective-permute-done.13 = bf16[128,1152]{1,0:T(8,128)(2,1)S(1)} collective-permute-done((bf16[128,1152]{1,0:T(8,128)(2,1)S(1)}, bf16[128,1152]{1,0:T(8,128)(2,1)S(1)}, u32[]{:S(2)}, u32[]{:S(2)}) %collective-permute-start.13) | collective-permute-done | bytes 294944 | tf_op jit(solution)/shard_map/ppermute | solution.py:23
  302.6 6.7 collective-permute-done.17
  314.3 4.3 convolution_convert_fusion.2
  318.6 8.4 %multiply_convert_fusion = (bf16[512,1728]{0,1:T(8,128)(2,1)S(1)}, bf16[512,1728]{0,1:T(8,128)(2,1)S(1)}) fusion(f32[512,1728]{0,1:T(8,128)S(1)} %copy-done.77, f32[512,1728]{0,1:T(8,128)} %get-tuple-element.185, bf16[1728,1152]{0,1:T(8,128)(2,1)S(1)} %copy-done.67, bf16[128,1152]{1,0:T(8,128)(2,1)S(1)} %collective-permute-done.17, ...), kind=kOutput, calls=%fused_computation.20 | convolution fusion | flops 2064384000 | bytes 15777792 | tf_op jit(solution)/shard_map/ld,fd->lf/dot_general | solution.py:220
  329.7 5.4 convolution_convert_fusion.1
  335.1 5.3 convolution_convert_fusion
  344.1 6.5 copy.60
  350.7 6.5 copy.62
  362.7 6.5 copy.64
  369.3 7.4 %collective-permute-done.19 = bf16[128,1152]{1,0:T(8,128)(2,1)} collective-permute-done((bf16[128,1152]{1,0:T(8,128)(2,1)}, bf16[128,1152]{1,0:T(8,128)(2,1)}, u32[]{:S(2)}, u32[]{:S(2)}) %collective-permute-start.19) | collective-permute-done | bytes 294944 | tf_op jit(solution)/shard_map/ppermute | solution.py:23
  383.5 4.8 collective-permute-done.21
  388.4 6.7 collective-permute-done.22
  403.9 13.6 %collective-permute-done.24 = bf16[512,256]{1,0:T(8,128)(2,1)S(1)} collective-permute-done((bf16[512,256]{1,0:T(8,128)(2,1)S(1)}, bf16[512,256]{1,0:T(8,128)(2,1)S(1)}, u32[]{:S(2)}, u32[]{:S(2)}) %collective-permute-start.24) | collective-permute-done | bytes 262176 | tf_op jit(solution)/shard_map/ppermute | solution.py:18
  442.2 4.5 reduce-scatter.13.cloned.1.call-done
  449.0 89.0 %reduce-scatter.15.cloned.1.call-done = bf16[144,1728]{1,0:T(8,128)(2,1)} async-done(((bf16[1152,1728]{1,0:T(8,128)(2,1)}), bf16[144,1728]{1,0:T(8,128)(2,1)}) %reduce-scatter.15.cloned.1.call-update) | async-done | bytes 497680
  540.3 88.5 %reduce-scatter.17.cloned.1.call-done = bf16[144,1728]{1,0:T(8,128)(2,1)} async-done(((bf16[1152,1728]{1,0:T(8,128)(2,1)}), bf16[144,1728]{1,0:T(8,128)(2,1)}) %reduce-scatter.17.cloned.1.call-update) | async-done | bytes 497680
  642.1 62.7 %reduce-scatter.19.cloned.1.call-done = bf16[144,1152]{1,0:T(8,128)(2,1)} async-done(((bf16[1152,1152]{1,0:T(8,128)(2,1)}), bf16[144,1152]{1,0:T(8,128)(2,1)}) %reduce-scatter.19.cloned.1.call-update) | async-done | bytes 331792
  713.0 10.0 %collective-permute-done.30 = bf16[144,640]{0,1:T(8,128)(2,1)S(1)} collective-permute-done((bf16[144,640]{0,1:T(8,128)(2,1)S(1)}, bf16[144,640]{0,1:T(8,128)(2,1)S(1)}, u32[]{:S(2)}, u32[]{:S(2)}) %collective-permute-start.30) | collective-permute-done | bytes 184352 | tf_op jit(solution)/shard_map/ppermute | solution.py:23
  (352 shorter events, 128.2 us)
Async XLA Ops:
  7.2 63.9 %all-gather.4.cloned.1.call-start = ((), (), s32[]{:S(2)}) async-start(), calls=%async_computation.4 | async-start | bytes 2985984 | tf_op jit(solution)/shard_map/all_gather | solution.py:138
  13.2 191.2 %all-gather.6.cloned.1.call-start = ((), (), s32[]{:S(2)}) async-start(), calls=%async_computation.5 | async-start | bytes 9289728 | tf_op jit(solution)/shard_map/all_gather | solution.py:139
  13.9 263.5 %all-gather.8.cloned.1.call-start = ((), (), s32[]{:S(2)}) async-start(), calls=%async_computation.6 | async-start | bytes 4644864 | tf_op jit(solution)/shard_map/all_gather | solution.py:140
  74.2 372.5 %reduce-scatter.13.cloned.1.call-start = ((), (), s32[]{:S(2)}) async-start(), calls=%async_computation.7 | async-start | bytes 4644864
  74.5 15.0 %collective-permute-start.2 = (bf16[128,1152]{1,0:T(8,128)(2,1)S(1)}, bf16[128,1152]{1,0:T(8,128)(2,1)S(1)}, u32[]{:S(2)}, u32[]{:S(2)}) collective-permute-start(bf16[128,1152]{1,0:T(8,128)(2,1)S(1)} %get-tuple-element.141), channel_id=1, source_target_pairs={{0,2},{1,3},{2,0},{3,1},{4,6},{5,7},{6,4},{7,5},{8,10},{9,11},{10,... | collective-permute-start | bytes 884744 | tf_op jit(solution)/shard_map/ppermute | solution.py:23
  76.0 13.8 %collective-permute-start.3 = (bf16[128,1152]{1,0:T(8,128)(2,1)S(1)}, bf16[128,1152]{1,0:T(8,128)(2,1)S(1)}, u32[]{:S(2)}, u32[]{:S(2)}) collective-permute-start(bf16[128,1152]{1,0:T(8,128)(2,1)S(1)} %get-tuple-element.141), channel_id=1, source_target_pairs={{0,1},{1,2},{2,3},{3,0},{4,5},{5,6},{6,7},{7,4},{8,9},{9,10},{10,1... | collective-permute-start | bytes 884744 | tf_op jit(solution)/shard_map/ppermute | solution.py:23
  94.9 18.2 %collective-permute-start.4 = (bf16[512,256]{1,0:T(8,128)(2,1)S(1)}, bf16[512,256]{1,0:T(8,128)(2,1)S(1)}, u32[]{:S(2)}, u32[]{:S(2)}) collective-permute-start(bf16[512,256]{1,0:T(8,128)(2,1)S(1)} %pad_maximum_fusion.9), channel_id=1, source_target_pairs={{0,4},{4,8},{8,12},{12,16},{16,20},{20,24},{24,28},{1,5},{5,9},{9,... | collective-permute-start | bytes 786440 | tf_op jit(solution)/shard_map/ppermute | solution.py:18
  103.1 13.9 %collective-permute-start.5 = (bf16[512,256]{1,0:T(8,128)(2,1)S(1)}, bf16[512,256]{1,0:T(8,128)(2,1)S(1)}, u32[]{:S(2)}, u32[]{:S(2)}) collective-permute-start(bf16[512,256]{1,0:T(8,128)(2,1)S(1)} %slice.321), channel_id=1, source_target_pairs={{0,4},{4,8},{8,12},{12,16},{16,20},{20,24},{24,28},{1,5},{5,9},{9,... | collective-permute-start | bytes 786440 | tf_op jit(solution)/shard_map/ppermute | solution.py:18
  119.6 14.6 %collective-permute-start.7 = (bf16[128,1152]{1,0:T(8,128)(2,1)S(1)}, bf16[128,1152]{1,0:T(8,128)(2,1)S(1)}, u32[]{:S(2)}, u32[]{:S(2)}) collective-permute-start(bf16[128,1152]{1,0:T(8,128)(2,1)S(1)} %get-tuple-element.159), channel_id=1, source_target_pairs={{0,2},{1,3},{2,0},{3,1},{4,6},{5,7},{6,4},{7,5},{8,10},{9,11},{10,... | collective-permute-start | bytes 884744 | tf_op jit(solution)/shard_map/ppermute | solution.py:23
  120.6 14.1 %collective-permute-start.6 = (bf16[128,1152]{1,0:T(8,128)(2,1)S(1)}, bf16[128,1152]{1,0:T(8,128)(2,1)S(1)}, u32[]{:S(2)}, u32[]{:S(2)}) collective-permute-start(bf16[128,1152]{1,0:T(8,128)(2,1)S(1)} %get-tuple-element.157), channel_id=1, source_target_pairs={{0,1},{1,2},{2,3},{3,0},{4,5},{5,6},{6,7},{7,4},{8,9},{9,10},{10,1... | collective-permute-start | bytes 884744 | tf_op jit(solution)/shard_map/ppermute | solution.py:23
  135.5 13.1 %collective-permute-start.11 = (bf16[128,1152]{1,0:T(8,128)(2,1)S(1)}, bf16[128,1152]{1,0:T(8,128)(2,1)S(1)}, u32[]{:S(2)}, u32[]{:S(2)}) collective-permute-start(bf16[128,1152]{1,0:T(8,128)(2,1)S(1)} %multiply_convert_fusion.3), channel_id=1, source_target_pairs={{0,1},{1,2},{2,3},{3,0},{4,5},{5,6},{6,7},{7,4},{8,9},{9,10},{10,1... | collective-permute-start | bytes 884744 | tf_op jit(solution)/shard_map/ppermute | solution.py:23
  135.5 13.1 %collective-permute-start.10 = (bf16[128,1152]{1,0:T(8,128)(2,1)S(1)}, bf16[128,1152]{1,0:T(8,128)(2,1)S(1)}, u32[]{:S(2)}, u32[]{:S(2)}) collective-permute-start(bf16[128,1152]{1,0:T(8,128)(2,1)S(1)} %multiply_convert_fusion.3), channel_id=1, source_target_pairs={{0,2},{1,3},{2,0},{3,1},{4,6},{5,7},{6,4},{7,5},{8,10},{9,11},{10,... | collective-permute-start | bytes 884744 | tf_op jit(solution)/shard_map/ppermute | solution.py:23
  136.7 16.2 %collective-permute-start.9 = (bf16[128,1152]{1,0:T(8,128)(2,1)S(1)}, bf16[128,1152]{1,0:T(8,128)(2,1)}, u32[]{:S(2)}, u32[]{:S(2)}) collective-permute-start(bf16[128,1152]{1,0:T(8,128)(2,1)S(1)} %multiply_convert_fusion.3), channel_id=1, source_target_pairs={{0,3},{1,0},{2,1},{3,2},{4,7},{5,4},{6,5},{7,6},{8,11},{9,8},{10,9... | collective-permute-start | bytes 884744 | tf_op jit(solution)/shard_map/ppermute | solution.py:23
  282.9 15.5 %collective-permute-start.13 = (bf16[128,1152]{1,0:T(8,128)(2,1)S(1)}, bf16[128,1152]{1,0:T(8,128)(2,1)S(1)}, u32[]{:S(2)}, u32[]{:S(2)}) collective-permute-start(bf16[128,1152]{1,0:T(8,128)(2,1)S(1)} %get-tuple-element.156), channel_id=1, source_target_pairs={{0,2},{1,3},{2,0},{3,1},{4,6},{5,7},{6,4},{7,5},{8,10},{9,11},{10,... | collective-permute-start | bytes 884744 | tf_op jit(solution)/shard_map/ppermute | solution.py:23
  284.4 14.1 %collective-permute-start.12 = (bf16[128,1152]{1,0:T(8,128)(2,1)S(1)}, bf16[128,1152]{1,0:T(8,128)(2,1)S(1)}, u32[]{:S(2)}, u32[]{:S(2)}) collective-permute-start(bf16[128,1152]{1,0:T(8,128)(2,1)S(1)} %get-tuple-element.154), channel_id=1, source_target_pairs={{0,1},{1,2},{2,3},{3,0},{4,5},{5,6},{6,7},{7,4},{8,9},{9,10},{10,1... | collective-permute-start | bytes 884744 | tf_op jit(solution)/shard_map/ppermute | solution.py:23
  300.6 9.9 %collective-permute-start.16 = (bf16[128,1152]{1,0:T(8,128)(2,1)S(1)}, bf16[128,1152]{1,0:T(8,128)(2,1)S(1)}, u32[]{:S(2)}, u32[]{:S(2)}) collective-permute-start(bf16[128,1152]{1,0:T(8,128)(2,1)S(1)} %get-tuple-element.160), channel_id=1, source_target_pairs={{0,2},{1,3},{2,0},{3,1},{4,6},{5,7},{6,4},{7,5},{8,10},{9,11},{10,... | collective-permute-start | bytes 884744 | tf_op jit(solution)/shard_map/ppermute | solution.py:23
  301.1 13.1 %collective-permute-start.15 = (bf16[128,1152]{1,0:T(8,128)(2,1)S(1)}, bf16[128,1152]{1,0:T(8,128)(2,1)S(1)}, u32[]{:S(2)}, u32[]{:S(2)}) collective-permute-start(bf16[128,1152]{1,0:T(8,128)(2,1)S(1)} %get-tuple-element.160), channel_id=1, source_target_pairs={{0,3},{1,0},{2,1},{3,2},{4,7},{5,4},{6,5},{7,6},{8,11},{9,8},{10,9... | collective-permute-start | bytes 884744 | tf_op jit(solution)/shard_map/ppermute | solution.py:23
  350.6 187.4 %reduce-scatter.15.cloned.1.call-start = ((), (), s32[]{:S(2)}) async-start(), calls=%async_computation.8 | async-start | bytes 4644864
  357.2 271.6 %reduce-scatter.17.cloned.1.call-start = ((), (), s32[]{:S(2)}) async-start(), calls=%async_computation.9 | async-start | bytes 4644864
  359.4 9.9 %collective-permute-start.20 = (bf16[128,1152]{1,0:T(8,128)(2,1)}, bf16[128,1152]{1,0:T(8,128)(2,1)}, u32[]{:S(2)}, u32[]{:S(2)}) collective-permute-start(bf16[128,1152]{1,0:T(8,128)(2,1)} %get-tuple-element.152), channel_id=1, source_target_pairs={{0,3},{1,0},{2,1},{3,2},{4,7},{5,4},{6,5},{7,6},{8,11},{9,8},{10,9... | collective-permute-start | bytes 884744 | tf_op jit(solution)/shard_map/ppermute | solution.py:23
  361.2 15.4 %collective-permute-start.19 = (bf16[128,1152]{1,0:T(8,128)(2,1)}, bf16[128,1152]{1,0:T(8,128)(2,1)}, u32[]{:S(2)}, u32[]{:S(2)}) collective-permute-start(bf16[128,1152]{1,0:T(8,128)(2,1)} %get-tuple-element.153), channel_id=1, source_target_pairs={{0,2},{1,3},{2,0},{3,1},{4,6},{5,7},{6,4},{7,5},{8,10},{9,11},{10,... | collective-permute-start | bytes 884744 | tf_op jit(solution)/shard_map/ppermute | solution.py:23
  362.7 14.0 %collective-permute-start.18 = (bf16[128,1152]{1,0:T(8,128)(2,1)}, bf16[128,1152]{1,0:T(8,128)(2,1)}, u32[]{:S(2)}, u32[]{:S(2)}) collective-permute-start(bf16[128,1152]{1,0:T(8,128)(2,1)} %get-tuple-element.151), channel_id=1, source_target_pairs={{0,1},{1,2},{2,3},{3,0},{4,5},{5,6},{6,7},{7,4},{8,9},{9,10},{10,1... | collective-permute-start | bytes 884744 | tf_op jit(solution)/shard_map/ppermute | solution.py:23
  369.2 335.6 %reduce-scatter.19.cloned.1.call-start = ((), (), s32[]{:S(2)}) async-start(), calls=%async_computation.10 | async-start | bytes 2985984
  381.2 13.9 %collective-permute-start.22 = (bf16[128,1152]{1,0:T(8,128)(2,1)S(1)}, bf16[128,1152]{1,0:T(8,128)(2,1)S(1)}, u32[]{:S(2)}, u32[]{:S(2)}) collective-permute-start(bf16[128,1152]{1,0:T(8,128)(2,1)S(1)} %get-tuple-element.132), channel_id=1, source_target_pairs={{0,2},{1,3},{2,0},{3,1},{4,6},{5,7},{6,4},{7,5},{8,10},{9,11},{10,... | collective-permute-start | bytes 884744 | tf_op jit(solution)/shard_map/ppermute | solution.py:23
  382.0 14.1 %collective-permute-start.23 = (bf16[128,1152]{1,0:T(8,128)(2,1)S(1)}, bf16[128,1152]{1,0:T(8,128)(2,1)S(1)}, u32[]{:S(2)}, u32[]{:S(2)}) collective-permute-start(bf16[128,1152]{1,0:T(8,128)(2,1)S(1)} %get-tuple-element.132), channel_id=1, source_target_pairs={{0,1},{1,2},{2,3},{3,0},{4,5},{5,6},{6,7},{7,4},{8,9},{9,10},{10,1... | collective-permute-start | bytes 884744 | tf_op jit(solution)/shard_map/ppermute | solution.py:23
  397.2 22.5 %collective-permute-start.25 = (bf16[512,256]{1,0:T(8,128)(2,1)S(1)}, bf16[512,256]{1,0:T(8,128)(2,1)S(1)}, u32[]{:S(2)}, u32[]{:S(2)}) collective-permute-start(bf16[512,256]{1,0:T(8,128)(2,1)S(1)} %slice.319), channel_id=1, source_target_pairs={{4,0},{8,4},{12,8},{16,12},{20,16},{24,20},{28,24},{5,1},{9,5},{13... | collective-permute-start | bytes 786440 | tf_op jit(solution)/shard_map/ppermute | solution.py:18
  400.7 16.8 %collective-permute-start.24 = (bf16[512,256]{1,0:T(8,128)(2,1)S(1)}, bf16[512,256]{1,0:T(8,128)(2,1)S(1)}, u32[]{:S(2)}, u32[]{:S(2)}) collective-permute-start(bf16[512,256]{1,0:T(8,128)(2,1)S(1)} %slice.320), channel_id=1, source_target_pairs={{4,0},{8,4},{12,8},{16,12},{20,16},{24,20},{28,24},{5,1},{9,5},{13... | collective-permute-start | bytes 786440 | tf_op jit(solution)/shard_map/ppermute | solution.py:18
  421.6 11.8 %collective-permute-start.28 = (bf16[128,1152]{1,0:T(8,128)(2,1)S(1)}, bf16[128,1152]{1,0:T(8,128)(2,1)S(1)}, u32[]{:S(2)}, u32[]{:S(2)}) collective-permute-start(bf16[128,1152]{1,0:T(8,128)(2,1)S(1)} %get-tuple-element.149), channel_id=1, source_target_pairs={{0,3},{1,0},{2,1},{3,2},{4,7},{5,4},{6,5},{7,6},{8,11},{9,8},{10,9... | collective-permute-start | bytes 884744 | tf_op jit(solution)/shard_map/ppermute | solution.py:23
  421.6 13.9 %collective-permute-start.27 = (bf16[128,1152]{1,0:T(8,128)(2,1)S(1)}, bf16[128,1152]{1,0:T(8,128)(2,1)S(1)}, u32[]{:S(2)}, u32[]{:S(2)}) collective-permute-start(bf16[128,1152]{1,0:T(8,128)(2,1)S(1)} %get-tuple-element.150), channel_id=1, source_target_pairs={{0,2},{1,3},{2,0},{3,1},{4,6},{5,7},{6,4},{7,5},{8,10},{9,11},{10,... | collective-permute-start | bytes 884744 | tf_op jit(solution)/shard_map/ppermute | solution.py:23
  422.4 14.2 %collective-permute-start.26 = (bf16[128,1152]{1,0:T(8,128)(2,1)S(1)}, bf16[128,1152]{1,0:T(8,128)(2,1)}, u32[]{:S(2)}, u32[]{:S(2)}) collective-permute-start(bf16[128,1152]{1,0:T(8,128)(2,1)S(1)} %get-tuple-element.148), channel_id=1, source_target_pairs={{0,1},{1,2},{2,3},{3,0},{4,5},{5,6},{6,7},{7,4},{8,9},{9,10},{10,1... | collective-permute-start | bytes 884744 | tf_op jit(solution)/shard_map/ppermute | solution.py:23
  706.0 17.0 %collective-permute-start.30 = (bf16[144,640]{0,1:T(8,128)(2,1)S(1)}, bf16[144,640]{0,1:T(8,128)(2,1)S(1)}, u32[]{:S(2)}, u32[]{:S(2)}) collective-permute-start(bf16[144,640]{0,1:T(8,128)(2,1)S(1)} %copy.69), channel_id=1, source_target_pairs={{0,2},{1,3},{2,0},{3,1},{4,6},{5,7},{6,4},{7,5},{8,10},{9,11},{10,... | collective-permute-start | bytes 552968 | tf_op jit(solution)/shard_map/ppermute | solution.py:23
  707.5 15.5 %collective-permute-start.29 = (bf16[144,640]{0,1:T(8,128)(2,1)S(1)}, bf16[144,640]{0,1:T(8,128)(2,1)S(1)}, u32[]{:S(2)}, u32[]{:S(2)}) collective-permute-start(bf16[144,640]{0,1:T(8,128)(2,1)S(1)} %copy.69), channel_id=1, source_target_pairs={{0,1},{1,2},{2,3},{3,0},{4,5},{5,6},{6,7},{7,4},{8,9},{9,10},{10,1... | collective-permute-start | bytes 552968 | tf_op jit(solution)/shard_map/ppermute | solution.py:23
  (89 other events, 828.1 us)
Sparse Core Ops, SparseCore 0:
  13.3 57.7 all-gather.3
  73.3 131.1 all-gather.5
  206.6 70.7 all-gather.7
  350.7 95.9 reduce-scatter.12
  450.5 87.4 reduce-scatter.14
  541.4 87.2 reduce-scatter.16
  634.5 70.2 reduce-scatter.18

commit v2 on v1

--- a/solution.py
+++ b/solution.py
@@ -56,6 +56,49 @@
             for step in range(count)
         ]
     )
+
+
+def swap_pairs(value):
+    count = lax.axis_size("dp")
+    return lax.ppermute(value, "dp", [(i, i + 1 - 2 * (i % 2)) for i in range(count)])
+
+
+def gather_dp(value):
+    half = lax.axis_size("dp") // 2
+    me = lax.axis_index("dp")
+    other = swap_pairs(value)
+    pair = jnp.where(
+        lax.rem(me, 2) == 0,
+        jnp.concatenate([value, other], axis=0),
+        jnp.concatenate([other, value], axis=0),
+    )
+    rows = pair.shape[0]
+    whole = jnp.zeros((half * rows,) + value.shape[1:], value.dtype)
+    for step in range(half):
+        block = pair if step == 0 else shifted(pair, "dp", -2 * step)
+        owner = lax.rem(me // 2 + step, half)
+        whole = lax.dynamic_update_slice_in_dim(whole, block, owner * rows, axis=0)
+    return whole
+
+
+def scatter_dp(value):
+    half = lax.axis_size("dp") // 2
+    me = lax.axis_index("dp")
+    parity = lax.rem(me, 2)
+    split = value.reshape((half, 2, -1) + value.shape[1:])
+    kept = lax.dynamic_index_in_dim(split, parity, axis=1, keepdims=False)
+    sent = lax.dynamic_index_in_dim(split, 1 - parity, axis=1, keepdims=False)
+    part = kept.astype(jnp.float32) + swap_pairs(sent).astype(jnp.float32)
+    blocks = [
+        lax.dynamic_index_in_dim(part, lax.rem(me // 2 + step, half), axis=0, keepdims=False)
+        for step in range(half)
+    ]
+    total = blocks[0]
+    for step in range(1, half):
+        total = total + shifted(blocks[step].astype(value.dtype), "dp", 2 * step).astype(
+            jnp.float32
+        )
+    return total
 
 
 def split_rows(value):
@@ -135,9 +178,9 @@
     packed = jnp.concatenate(
         [q_weight, kv_weight, jnp.transpose(o_weight), gain_columns], axis=1
     )
-    packed_full = lax.all_gather(packed, "dp", axis=0, tiled=True)
+    packed_full = gather_dp(packed)
     gate_up_full = lax.all_gather(gate_up_weight, "dp", axis=1, tiled=True)
-    down_full = lax.all_gather(down_weight, "dp", axis=1, tiled=True)
+    down_turned = gather_dp(jnp.transpose(down_weight))
     joint_weight = packed_full[:, : 3 * head_size]
     output_turned = packed_full[:, 3 * head_size : 4 * head_size]
     gain_block = jnp.transpose(packed_full[:, 4 * head_size :]).astype(jnp.float32)
@@ -210,18 +253,21 @@
     hidden = gated_units(gate, up_part).astype(jnp.bfloat16)
     ff_out = scatter_relative(
         split_rows(
-            jnp.dot(hidden, down_full, preferred_element_type=jnp.float32).astype(jnp.bfloat16)
+            jnp.einsum(
+                "lf,df->ld", hidden, down_turned, preferred_element_type=jnp.float32
+            ).astype(jnp.bfloat16)
         )
     )
     result = (middle + normalize(ff_out, gains[3])).astype(jnp.bfloat16)
     top_grad = out_grad.astype(jnp.float32)
     ff_out_grad, ff_post_grad = norm_back(ff_out, gains[3], top_grad)
     ff_grad_all = jnp.concatenate(gather_relative(ff_out_grad.astype(jnp.bfloat16)), axis=0)
+    down_low = jnp.einsum(
+        "ld,lf->df", ff_grad_all, hidden, preferred_element_type=jnp.float32
+    ).astype(jnp.bfloat16)
+    ff_grad_all, down_low = lax.optimization_barrier((ff_grad_all, down_low))
     hidden_grad = jnp.einsum(
-        "ld,fd->lf", ff_grad_all, down_full, preferred_element_type=jnp.float32
-    )
-    down_grad_turned = jnp.einsum(
-        "ld,lf->df", ff_grad_all, hidden, preferred_element_type=jnp.float32
+        "ld,df->lf", ff_grad_all, down_turned, preferred_element_type=jnp.float32
     )
     unused, unit_pull = jax.vjp(gated_units, gate, up_part)
     gate_grad, up_grad = unit_pull(hidden_grad)
@@ -233,17 +279,16 @@
         jnp.einsum("lf,df->ld", gate_low, gate_up_full[0], preferred_element_type=jnp.float32)
         + jnp.einsum("lf,df->ld", up_low, gate_up_full[1], preferred_element_type=jnp.float32)
     ).astype(jnp.bfloat16)
-    ff_in_partial, down_low, gate_turned_low, up_turned_low = lax.optimization_barrier(
+    ff_in_partial, gate_turned_low, up_turned_low = lax.optimization_barrier(
         (
             ff_in_partial,
-            down_grad_turned.astype(jnp.bfloat16),
             gate_turned.astype(jnp.bfloat16),
             up_turned.astype(jnp.bfloat16),
         )
     )
-    feed_forward_owned = tuple(
+    gate_up_parts = tuple(
         lax.psum_scatter(item, "dp", scatter_dimension=0, tiled=True)
-        for item in (down_low, gate_turned_low, up_turned_low)
+        for item in (gate_turned_low, up_turned_low)
     )
     ff_in_grad = scatter_relative(split_rows(ff_in_partial))
     middle_part, ff_pre_grad = norm_back(middle, gains[2], ff_in_grad)
@@ -327,15 +372,12 @@
         ],
         axis=1,
     )
-    packed_grad, feed_forward_owned = lax.optimization_barrier(
-        (packed_grad, feed_forward_owned)
-    )
-    down_owned = jnp.transpose(feed_forward_owned[0]).astype(jnp.float32)
-    gate_up_owned = jnp.stack(feed_forward_owned[1:], axis=0).astype(jnp.float32)
-    packed_owned = lax.psum_scatter(packed_grad, "dp", scatter_dimension=0, tiled=True)
+    down_owned = jnp.transpose(scatter_dp(down_low))
+    gate_up_owned = jnp.stack(gate_up_parts, axis=0).astype(jnp.float32)
+    packed_owned = scatter_dp(packed_grad)
     query_owned = packed_owned[:, :head_size].astype(jnp.float32)
     output_owned = jnp.transpose(packed_owned[:, head_size : 2 * head_size]).astype(jnp.float32)
-    summed = sum_over_mp(packed_owned[:, 2 * head_size :])
+    summed = sum_over_mp(packed_owned[:, 2 * head_size :].astype(jnp.bfloat16))
     keyval_owned = summed[:, : 2 * head_size]
     gain_owned = jnp.transpose(summed[:, 2 * head_size :])
     return (

time: 740 us -> 684 us (0.924)
  waiting for transfers between devices: 522 us -> 346 us
  local copies, waits for them, and re-layouts: 65.8 us -> 139 us
  starting transfers between devices: 46.7 us -> 73.1 us
  other arithmetic: 22.5 us -> 34.5 us
    unnamed x11 -> x5, waiting for transfers between devices: 246 us -> 0.72 us
    ppermute x27 -> x39, waiting for transfers between devices: 91.2 us -> 246 us  [shifted(): lax.ppermute(value, axis, [(i, (i + shift) % count) for i in range(count)])]
    all_gather x2 -> x0, waiting for transfers between devices: 116 us -> none  [the longest x1 59.2 us: local(): down_full = lax.all_gather(down_weight, 'dp', axis=1, tiled=True)]
    all_gather x1, waiting for transfers between devices: 51.6 us -> 0.01 us  [local(): gate_up_full = lax.all_gather(gate_up_weight, 'dp', axis=1, tiled=True)]
    dynamic_update_slice x0 -> x7, local copies, waits for them, and re-layouts: none -> 48.4 us  [gather_dp(): whole = lax.dynamic_update_slice_in_dim(whole, block, owner * rows, axis=0)]
    ppermute x0 -> x4, waiting for transfers between devices: none -> 43.2 us  [swap_pairs(): lax.ppermute(value, 'dp', [(i, i + 1 - 2 * (i % 2)) for i in range(count)])]
    ppermute x5, waiting for transfers between devices: 17.2 us -> 56.6 us  [from_behind(): lax.ppermute(value, axis, [(source, source + steps) for source in range(l...]
    ppermute x27 -> x39, starting transfers between devices: 27 us -> 55.8 us  [shifted(): lax.ppermute(value, axis, [(i, (i + shift) % count) for i in range(count)])]
  transfers between devices with their start and end apart: 39 -> 51, of which waited for: 32 -> 24; matrix products, arithmetic and copies ran while one was open for 11% -> 24% of each run, Pallas kernels for 0% -> 0%
where the time goes in v2:
time: 684 us; the launch traced here: 673 us
  waiting for transfers between devices  346 us (51%)
  local copies, waits for them, and re-layouts  139 us (20%)
  starting transfers between devices  73.1 us (11%)
  matrix products  65.1 us (10%)
  other arithmetic  34.5 us (5%)
  between operations  15.5 us (2%)
    ppermute x39, waiting for transfers between devices, shifted(): lax.ppermute(value, axis, [(i, (i + shift) % count) for i in range(count)])  246 us
    ppermute x5, waiting for transfers between devices, from_behind(): lax.ppermute(value, axis, [(source, source + steps) for source in range(l...  56.6 us
    ppermute x39, starting transfers between devices, shifted(): lax.ppermute(value, axis, [(i, (i + shift) % count) for i in range(count)])  55.8 us
    dynamic_update_slice x7, local copies, waits for them, and re-layouts, gather_dp(): whole = lax.dynamic_update_slice_in_dim(whole, block, owner * rows, axis=0)  48.4 us
    ppermute x4, waiting for transfers between devices, swap_pairs(): lax.ppermute(value, 'dp', [(i, i + 1 - 2 * (i % 2)) for i in range(count)])  43.2 us
    unnamed x168, local copies, waits for them, and re-layouts  27.7 us
    dot_general x1, matrix products, local(): jnp.einsum('ld,df->lf', ff_grad_all, down_turned, preferred_element_type=...  16.3 us
  transfers between devices with their start and end apart: 51, of which 24 were waited for; matrix products, arithmetic and copies ran while one was open for 24% of the time, Pallas kernels for 0%

profile of v2, /device:TPU:0, one launch (start us, length us, event | category | flops | bytes accessed | tf_op | source)
XLA Modules:
  0.0 673.0 jit_solution(2199567405516949418)
XLA Ops:
  16.2 9.5 %collective-permute-done.1 = bf16[144,1152]{1,0:T(8,128)(2,1)S(1)} collective-permute-done((bf16[144,1152]{1,0:T(8,128)(2,1)S(1)}, bf16[144,1152]{1,0:T(8,128)(2,1)S(1)}, u32[]{:S(2)}, u32[]{:S(2)}) %collective-permute-start.1) | collective-permute-done | bytes 331808 | tf_op jit(solution)/shard_map/ppermute | solution.py:63
  32.4 4.4 collective-permute-start
  41.1 10.5 %dynamic_update_slice.48 = bf16[1152,1152]{0,1:T(8,128)(2,1)S(1)} dynamic-update-slice(bf16[1152,1152]{0,1:T(8,128)(2,1)S(1)} %broadcast_in_dim.21, bf16[288,1152]{0,1:T(8,128)(2,1)} %copy.50, s32[]{:T(128)S(6)} %select_n.112, s32[]{:T(128)} %constant.218.clone.1) | dynamic-update-slice | bytes 1327108 | tf_op jit(solution)/shard_map/dynamic_update_slice | solution.py:80
  51.6 18.5 %collective-permute-done.2 = bf16[288,1152]{1,0:T(8,128)(2,1)} collective-permute-done((bf16[288,1152]{1,0:T(8,128)(2,1)}, bf16[288,1152]{1,0:T(8,128)(2,1)}, u32[]{:S(2)}, u32[]{:S(2)}) %collective-permute-start.2) | collective-permute-done | bytes 663584 | tf_op jit(solution)/shard_map/ppermute | solution.py:23
  72.4 11.7 %dynamic_update_slice.49 = bf16[1152,1152]{0,1:T(8,128)(2,1)S(1)} dynamic-update-slice(bf16[1152,1152]{0,1:T(8,128)(2,1)S(1)} %dynamic_update_slice.48, bf16[288,1152]{0,1:T(8,128)(2,1)} %copy.51, s32[]{:T(128)S(6)} %select_n.113, s32[]{:T(128)} %constant.218.clone.1) | dynamic-update-slice | bytes 1327108 | tf_op jit(solution)/shard_map/dynamic_update_slice | solution.py:80
  84.1 56.9 %collective-permute-done.3 = bf16[288,1152]{1,0:T(8,128)(2,1)} collective-permute-done((bf16[288,1152]{1,0:T(8,128)(2,1)}, bf16[288,1152]{1,0:T(8,128)(2,1)}, u32[]{:S(2)}, u32[]{:S(2)}) %collective-permute-start.3) | collective-permute-done | bytes 663584 | tf_op jit(solution)/shard_map/ppermute | solution.py:23
  143.3 11.6 %dynamic_update_slice.50 = bf16[1152,1152]{0,1:T(8,128)(2,1)S(1)} dynamic-update-slice(bf16[1152,1152]{0,1:T(8,128)(2,1)S(1)} %dynamic_update_slice.49, bf16[288,1152]{0,1:T(8,128)(2,1)} %copy.52, s32[]{:T(128)S(6)} %select_n.114, s32[]{:T(128)} %constant.218.clone.1) | dynamic-update-slice | bytes 1327108 | tf_op jit(solution)/shard_map/dynamic_update_slice | solution.py:80
  157.2 11.5 %dynamic_update_slice.51 = bf16[1152,1152]{0,1:T(8,128)(2,1)S(1)} dynamic-update-slice(bf16[1152,1152]{0,1:T(8,128)(2,1)S(1)} %dynamic_update_slice.50, bf16[288,1152]{0,1:T(8,128)(2,1)} %copy.53, s32[]{:T(128)S(6)} %select_n.115, s32[]{:T(128)} %constant.218.clone.1) | dynamic-update-slice | bytes 1327108 | tf_op jit(solution)/shard_map/dynamic_update_slice | solution.py:80
  212.4 23.8 %collective-permute-start.18 = (bf16[288,1728]{1,0:T(8,128)(2,1)S(1)}, bf16[288,1728]{1,0:T(8,128)(2,1)S(1)}, u32[]{:S(2)}, u32[]{:S(2)}) collective-permute-start(bf16[288,1728]{1,0:T(8,128)(2,1)S(1)} %get-tuple-element.137), channel_id=1, source_target_pairs={{0,16},{4,20},{8,24},{12,28},{16,0},{20,4},{24,8},{28,12},{1,17},{... | collective-permute-start | bytes 2985992 | tf_op jit(solution)/shard_map/ppermute | solution.py:23
  242.6 60.7 %collective-permute-done.18 = bf16[288,1728]{1,0:T(8,128)(2,1)S(1)} collective-permute-done((bf16[288,1728]{1,0:T(8,128)(2,1)S(1)}, bf16[288,1728]{1,0:T(8,128)(2,1)S(1)}, u32[]{:S(2)}, u32[]{:S(2)}) %collective-permute-start.18) | collective-permute-done | bytes 995360 | tf_op jit(solution)/shard_map/ppermute | solution.py:23
  306.9 5.2 fusion.2
  312.1 4.3 multiply_convert_fusion.1
  316.4 4.8 convolution_convert_fusion.5
  323.8 6.9 %collective-permute-done.22 = bf16[128,1152]{1,0:T(8,128)(2,1)S(1)} collective-permute-done((bf16[128,1152]{1,0:T(8,128)(2,1)S(1)}, bf16[128,1152]{1,0:T(8,128)(2,1)S(1)}, u32[]{:S(2)}, u32[]{:S(2)}) %collective-permute-start.22) | collective-permute-done | bytes 294944 | tf_op jit(solution)/shard_map/ppermute | solution.py:23
  330.7 6.9 %collective-permute-done.21 = bf16[128,1152]{1,0:T(8,128)(2,1)S(1)} collective-permute-done((bf16[128,1152]{1,0:T(8,128)(2,1)S(1)}, bf16[128,1152]{1,0:T(8,128)(2,1)S(1)}, u32[]{:S(2)}, u32[]{:S(2)}) %collective-permute-start.21) | collective-permute-done | bytes 294944 | tf_op jit(solution)/shard_map/ppermute | solution.py:23
  342.8 5.5 collective-permute-done.25
  349.4 5.1 collective-permute-done.23
  354.6 4.4 convolution_convert_fusion.2
  359.0 16.3 %multiply_convert_fusion = (bf16[512,1728]{0,1:T(8,128)(2,1)S(1)}, bf16[512,1728]{0,1:T(8,128)(2,1)S(1)}) fusion(f32[512,1728]{0,1:T(8,128)S(1)} %fusion.2, f32[512,1728]{0,1:T(8,128)S(1)} %get-tuple-element.187, bf16[512,1152]{1,0:T(8,128)(2,1)S(1)} %pad_maximum_fusion.1, bf16[1152,1728]{1,0:T(8,128)(2,1)} %constant_dynamic-update-slice_fusion.4), kind=kOutput, calls=%fused_computation.21 | convolution fusion | flops 2059665408 | bytes 15777792 | tf_op jit(solution)/shard_map/ld,df->lf/dot_general | solution.py:269
  377.9 5.3 convolution_convert_fusion.1
  383.2 5.4 convolution_convert_fusion
  388.6 3.7 fusion.13
  392.3 6.7 copy.66
  403.3 7.4 %collective-permute-done.28 = bf16[128,1152]{1,0:T(8,128)(2,1)} collective-permute-done((bf16[128,1152]{1,0:T(8,128)(2,1)}, bf16[128,1152]{1,0:T(8,128)(2,1)}, u32[]{:S(2)}, u32[]{:S(2)}) %collective-permute-start.28) | collective-permute-done | bytes 294944 | tf_op jit(solution)/shard_map/ppermute | solution.py:23
  410.7 6.6 collective-permute-done.27
  425.3 6.5 copy.59
  436.6 6.5 copy.64
  458.6 54.1 %collective-permute-done.32 = bf16[512,256]{1,0:T(8,128)(2,1)S(1)} collective-permute-done((bf16[512,256]{1,0:T(8,128)(2,1)S(1)}, bf16[512,256]{1,0:T(8,128)(2,1)S(1)}, u32[]{:S(2)}, u32[]{:S(2)}) %collective-permute-start.32) | collective-permute-done | bytes 262176 | tf_op jit(solution)/shard_map/ppermute | solution.py:18
  550.8 33.7 %collective-permute-done.37 = bf16[4,144,1152]{2,1,0:T(8,128)(2,1)S(1)} collective-permute-done((bf16[4,144,1152]{2,1,0:T(8,128)(2,1)S(1)}, bf16[4,144,1152]{2,1,0:T(8,128)(2,1)S(1)}, u32[]{:S(2)}, u32[]{:S(2)}) %collective-permute-start.37) | collective-permute-done | bytes 1327136 | tf_op jit(solution)/shard_map/ppermute | solution.py:63
  588.8 32.2 %collective-permute-done.46 = bf16[144,1728]{1,0:T(8,128)(2,1)S(1)} collective-permute-done((bf16[144,1728]{1,0:T(8,128)(2,1)S(1)}, bf16[144,1728]{1,0:T(8,128)(2,1)S(1)}, u32[]{:S(2)}, u32[]{:S(2)}) %collective-permute-start.46) | collective-permute-done | bytes 497696 | tf_op jit(solution)/shard_map/ppermute | solution.py:23
  622.2 21.5 %collective-permute-done.39 = bf16[144,1152]{1,0:T(8,128)(2,1)S(1)} collective-permute-done((bf16[144,1152]{1,0:T(8,128)(2,1)S(1)}, bf16[144,1152]{1,0:T(8,128)(2,1)S(1)}, u32[]{:S(2)}, u32[]{:S(2)}) %collective-permute-start.39) | collective-permute-done | bytes 331808 | tf_op jit(solution)/shard_map/ppermute | solution.py:23
  648.0 6.7 collective-permute-done.42
  (386 shorter events, 183.1 us)
Async XLA Ops:
  7.2 299.7 %all-gather.2.cloned.1.call-start = ((), (), s32[]{:S(2)}) async-start(), calls=%async_computation.2 | async-start | bytes 9289728 | tf_op jit(solution)/shard_map/all_gather | solution.py:182
  7.9 649.4 %reduce-scatter.9.cloned.1.call-start = ((), (), s32[]{:S(2)}) async-start(), calls=%async_computation.4 | async-start | bytes 4644864
  27.8 42.2 %collective-permute-start.2 = (bf16[288,1152]{1,0:T(8,128)(2,1)}, bf16[288,1152]{1,0:T(8,128)(2,1)}, u32[]{:S(2)}, u32[]{:S(2)}) collective-permute-start(bf16[288,1152]{1,0:T(8,128)(2,1)} %maximum_select_fusion.1), channel_id=1, source_target_pairs={{0,24},{4,28},{8,0},{12,4},{16,8},{20,12},{24,16},{28,20},{1,25},{... | collective-permute-start | bytes 1990664 | tf_op jit(solution)/shard_map/ppermute | solution.py:23
  31.5 109.5 %collective-permute-start.3 = (bf16[288,1152]{1,0:T(8,128)(2,1)}, bf16[288,1152]{1,0:T(8,128)(2,1)}, u32[]{:S(2)}, u32[]{:S(2)}) collective-permute-start(bf16[288,1152]{1,0:T(8,128)(2,1)} %maximum_select_fusion.1), channel_id=1, source_target_pairs={{0,16},{4,20},{8,24},{12,28},{16,0},{20,4},{24,8},{28,12},{1,17},{... | collective-permute-start | bytes 1990664 | tf_op jit(solution)/shard_map/ppermute | solution.py:23
  31.5 123.4 %collective-permute-start.4 = (bf16[288,1152]{1,0:T(8,128)(2,1)}, bf16[288,1152]{1,0:T(8,128)(2,1)}, u32[]{:S(2)}, u32[]{:S(2)}) collective-permute-start(bf16[288,1152]{1,0:T(8,128)(2,1)} %maximum_select_fusion.1), channel_id=1, source_target_pairs={{0,8},{4,12},{8,16},{12,20},{16,24},{20,28},{24,0},{28,4},{1,9},{5... | collective-permute-start | bytes 1990664 | tf_op jit(solution)/shard_map/ppermute | solution.py:23
  32.4 142.4 %collective-permute-start = (bf16[512]{0:T(512)(128)(2,1)S(1)}, bf16[512]{0:T(512)(128)(2,1)S(1)}, u32[]{:S(2)}, u32[]{:S(2)}) collective-permute-start(bf16[512]{0:T(512)(128)(2,1)S(1)} %add_convert_fusion.1), channel_id=1, source_target_pairs={{0,4},{4,8},{8,12},{12,16},{16,20},{20,24},{24,28},{1,5},{5,9},{9,... | collective-permute-start | bytes 3080 | tf_op jit(solution)/shard_map/ppermute | solution.py:18
  36.8 160.3 %collective-permute-start.16 = (bf16[144,1728]{1,0:T(8,128)(2,1)}, bf16[144,1728]{1,0:T(8,128)(2,1)}, u32[]{:S(2)}, u32[]{:S(2)}) collective-permute-start(bf16[144,1728]{1,0:T(8,128)(2,1)} %bitcast.4), channel_id=1, source_target_pairs={{0,4},{4,0},{8,12},{12,8},{16,20},{20,16},{24,28},{28,24},{1,5},{5... | collective-permute-start | bytes 1493000 | tf_op jit(solution)/shard_map/ppermute | solution.py:63
  202.2 34.0 %collective-permute-start.17 = (bf16[288,1728]{1,0:T(8,128)(2,1)S(1)}, bf16[288,1728]{1,0:T(8,128)(2,1)S(1)}, u32[]{:S(2)}, u32[]{:S(2)}) collective-permute-start(bf16[288,1728]{1,0:T(8,128)(2,1)S(1)} %get-tuple-element.137), channel_id=1, source_target_pairs={{0,24},{4,28},{8,0},{12,4},{16,8},{20,12},{24,16},{28,20},{1,25},{... | collective-permute-start | bytes 2985992 | tf_op jit(solution)/shard_map/ppermute | solution.py:23
  210.7 28.0 %collective-permute-start.12 = (bf16[128,1152]{1,0:T(8,128)(2,1)S(1)}, bf16[128,1152]{1,0:T(8,128)(2,1)S(1)}, u32[]{:S(2)}, u32[]{:S(2)}) collective-permute-start(bf16[128,1152]{1,0:T(8,128)(2,1)S(1)} %get-tuple-element.166), channel_id=1, source_target_pairs={{0,3},{1,0},{2,1},{3,2},{4,7},{5,4},{6,5},{7,6},{8,11},{9,8},{10,9... | collective-permute-start | bytes 884744 | tf_op jit(solution)/shard_map/ppermute | solution.py:23
  210.7 27.9 %collective-permute-start.11 = (bf16[128,1152]{1,0:T(8,128)(2,1)S(1)}, bf16[128,1152]{1,0:T(8,128)(2,1)S(1)}, u32[]{:S(2)}, u32[]{:S(2)}) collective-permute-start(bf16[128,1152]{1,0:T(8,128)(2,1)S(1)} %get-tuple-element.167), channel_id=1, source_target_pairs={{0,2},{1,3},{2,0},{3,1},{4,6},{5,7},{6,4},{7,5},{8,10},{9,11},{10,... | collective-permute-start | bytes 884744 | tf_op jit(solution)/shard_map/ppermute | solution.py:23
  212.2 26.4 %collective-permute-start.10 = (bf16[128,1152]{1,0:T(8,128)(2,1)S(1)}, bf16[128,1152]{1,0:T(8,128)(2,1)S(1)}, u32[]{:S(2)}, u32[]{:S(2)}) collective-permute-start(bf16[128,1152]{1,0:T(8,128)(2,1)S(1)} %get-tuple-element.165), channel_id=1, source_target_pairs={{0,1},{1,2},{2,3},{3,0},{4,5},{5,6},{6,7},{7,4},{8,9},{9,10},{10,1... | collective-permute-start | bytes 884744 | tf_op jit(solution)/shard_map/ppermute | solution.py:23
  212.4 90.9 %collective-permute-start.18 = (bf16[288,1728]{1,0:T(8,128)(2,1)S(1)}, bf16[288,1728]{1,0:T(8,128)(2,1)S(1)}, u32[]{:S(2)}, u32[]{:S(2)}) collective-permute-start(bf16[288,1728]{1,0:T(8,128)(2,1)S(1)} %get-tuple-element.137), channel_id=1, source_target_pairs={{0,16},{4,20},{8,24},{12,28},{16,0},{20,4},{24,8},{28,12},{1,17},{... | collective-permute-start | bytes 2985992 | tf_op jit(solution)/shard_map/ppermute | solution.py:23
  236.2 68.1 %collective-permute-start.19 = (bf16[288,1728]{1,0:T(8,128)(2,1)S(1)}, bf16[288,1728]{1,0:T(8,128)(2,1)S(1)}, u32[]{:S(2)}, u32[]{:S(2)}) collective-permute-start(bf16[288,1728]{1,0:T(8,128)(2,1)S(1)} %get-tuple-element.137), channel_id=1, source_target_pairs={{0,8},{4,12},{8,16},{12,20},{16,24},{20,28},{24,0},{28,4},{1,9},{5... | collective-permute-start | bytes 2985992 | tf_op jit(solution)/shard_map/ppermute | solution.py:23
  239.9 65.5 %collective-permute-start.15 = (bf16[128,1152]{1,0:T(8,128)(2,1)S(1)}, bf16[128,1152]{1,0:T(8,128)(2,1)S(1)}, u32[]{:S(2)}, u32[]{:S(2)}) collective-permute-start(bf16[128,1152]{1,0:T(8,128)(2,1)S(1)} %multiply_convert_fusion.3), channel_id=1, source_target_pairs={{0,1},{1,2},{2,3},{3,0},{4,5},{5,6},{6,7},{7,4},{8,9},{9,10},{10,1... | collective-permute-start | bytes 884744 | tf_op jit(solution)/shard_map/ppermute | solution.py:23
  240.7 64.8 %collective-permute-start.14 = (bf16[128,1152]{1,0:T(8,128)(2,1)S(1)}, bf16[128,1152]{1,0:T(8,128)(2,1)S(1)}, u32[]{:S(2)}, u32[]{:S(2)}) collective-permute-start(bf16[128,1152]{1,0:T(8,128)(2,1)S(1)} %multiply_convert_fusion.3), channel_id=1, source_target_pairs={{0,2},{1,3},{2,0},{3,1},{4,6},{5,7},{6,4},{7,5},{8,10},{9,11},{10,... | collective-permute-start | bytes 884744 | tf_op jit(solution)/shard_map/ppermute | solution.py:23
  241.4 65.5 %collective-permute-start.13 = (bf16[128,1152]{1,0:T(8,128)(2,1)S(1)}, bf16[128,1152]{1,0:T(8,128)(2,1)}, u32[]{:S(2)}, u32[]{:S(2)}) collective-permute-start(bf16[128,1152]{1,0:T(8,128)(2,1)S(1)} %multiply_convert_fusion.3), channel_id=1, source_target_pairs={{0,3},{1,0},{2,1},{3,2},{4,7},{5,4},{6,5},{7,6},{8,11},{9,8},{10,9... | collective-permute-start | bytes 884744 | tf_op jit(solution)/shard_map/ppermute | solution.py:23
  323.3 14.3 %collective-permute-start.21 = (bf16[128,1152]{1,0:T(8,128)(2,1)S(1)}, bf16[128,1152]{1,0:T(8,128)(2,1)S(1)}, u32[]{:S(2)}, u32[]{:S(2)}) collective-permute-start(bf16[128,1152]{1,0:T(8,128)(2,1)S(1)} %get-tuple-element.164), channel_id=1, source_target_pairs={{0,2},{1,3},{2,0},{3,1},{4,6},{5,7},{6,4},{7,5},{8,10},{9,11},{10,... | collective-permute-start | bytes 884744 | tf_op jit(solution)/shard_map/ppermute | solution.py:23
  399.0 260.6 %reduce-scatter.7.cloned.1.call-start = ((), (), s32[]{:S(2)}) async-start(), calls=%async_computation.3 | async-start | bytes 4644864
  424.7 20.7 %collective-permute-start.29 = (bf16[128,1152]{1,0:T(8,128)(2,1)}, bf16[128,1152]{1,0:T(8,128)(2,1)}, u32[]{:S(2)}, u32[]{:S(2)}) collective-permute-start(bf16[128,1152]{1,0:T(8,128)(2,1)} %get-tuple-element.132), channel_id=1, source_target_pairs={{0,3},{1,0},{2,1},{3,2},{4,7},{5,4},{6,5},{7,6},{8,11},{9,8},{10,9... | collective-permute-start | bytes 884744 | tf_op jit(solution)/shard_map/ppermute | solution.py:23
  431.8 14.6 %collective-permute-start.30 = (bf16[128,1152]{1,0:T(8,128)(2,1)}, bf16[128,1152]{1,0:T(8,128)(2,1)}, u32[]{:S(2)}, u32[]{:S(2)}) collective-permute-start(bf16[128,1152]{1,0:T(8,128)(2,1)} %get-tuple-element.132), channel_id=1, source_target_pairs={{0,2},{1,3},{2,0},{3,1},{4,6},{5,7},{6,4},{7,5},{8,10},{9,11},{10,... | collective-permute-start | bytes 884744 | tf_op jit(solution)/shard_map/ppermute | solution.py:23
  443.1 102.2 %collective-permute-start.44 = (bf16[4,144,1728]{2,1,0:T(8,128)(2,1)}, bf16[4,144,1728]{2,1,0:T(8,128)(2,1)}, u32[]{:S(2)}, u32[]{:S(2)}) collective-permute-start(bf16[4,144,1728]{2,1,0:T(8,128)(2,1)} %dynamic-slice_bitcast_fusion), channel_id=1, source_target_pairs={{0,4},{4,0},{8,12},{12,8},{16,20},{20,16},{24,28},{28,24},{1,5},{5... | collective-permute-start | bytes 5971976 | tf_op jit(solution)/shard_map/ppermute | solution.py:63
  453.3 61.7 %collective-permute-start.33 = (bf16[512,256]{1,0:T(8,128)(2,1)S(1)}, bf16[512,256]{1,0:T(8,128)(2,1)S(1)}, u32[]{:S(2)}, u32[]{:S(2)}) collective-permute-start(bf16[512,256]{1,0:T(8,128)(2,1)S(1)} %slice.326), channel_id=1, source_target_pairs={{4,0},{8,4},{12,8},{16,12},{20,16},{24,20},{28,24},{5,1},{9,5},{13... | collective-permute-start | bytes 786440 | tf_op jit(solution)/shard_map/ppermute | solution.py:18
  456.7 56.0 %collective-permute-start.32 = (bf16[512,256]{1,0:T(8,128)(2,1)S(1)}, bf16[512,256]{1,0:T(8,128)(2,1)S(1)}, u32[]{:S(2)}, u32[]{:S(2)}) collective-permute-start(bf16[512,256]{1,0:T(8,128)(2,1)S(1)} %slice.327), channel_id=1, source_target_pairs={{4,0},{8,4},{12,8},{16,12},{20,16},{24,20},{28,24},{5,1},{9,5},{13... | collective-permute-start | bytes 786440 | tf_op jit(solution)/shard_map/ppermute | solution.py:18
  518.0 14.7 %collective-permute-start.35 = (bf16[128,1152]{1,0:T(8,128)(2,1)S(1)}, bf16[128,1152]{1,0:T(8,128)(2,1)S(1)}, u32[]{:S(2)}, u32[]{:S(2)}) collective-permute-start(bf16[128,1152]{1,0:T(8,128)(2,1)S(1)} %get-tuple-element.158), channel_id=1, source_target_pairs={{0,2},{1,3},{2,0},{3,1},{4,6},{5,7},{6,4},{7,5},{8,10},{9,11},{10,... | collective-permute-start | bytes 884744 | tf_op jit(solution)/shard_map/ppermute | solution.py:23
  519.0 14.3 %collective-permute-start.34 = (bf16[128,1152]{1,0:T(8,128)(2,1)S(1)}, bf16[128,1152]{1,0:T(8,128)(2,1)}, u32[]{:S(2)}, u32[]{:S(2)}) collective-permute-start(bf16[128,1152]{1,0:T(8,128)(2,1)S(1)} %get-tuple-element.156), channel_id=1, source_target_pairs={{0,1},{1,2},{2,3},{3,0},{4,5},{5,6},{6,7},{7,4},{8,9},{9,10},{10,1... | collective-permute-start | bytes 884744 | tf_op jit(solution)/shard_map/ppermute | solution.py:23
  544.1 40.4 %collective-permute-start.37 = (bf16[4,144,1152]{2,1,0:T(8,128)(2,1)S(1)}, bf16[4,144,1152]{2,1,0:T(8,128)(2,1)S(1)}, u32[]{:S(2)}, u32[]{:S(2)}) collective-permute-start(bf16[4,144,1152]{2,1,0:T(8,128)(2,1)S(1)} %dynamic-slice_bitcast_fusion.1), channel_id=1, source_target_pairs={{0,4},{4,0},{8,12},{12,8},{16,20},{20,16},{24,28},{28,24},{1,5},{5... | collective-permute-start | bytes 3981320 | tf_op jit(solution)/shard_map/ppermute | solution.py:63
  547.5 39.4 %collective-permute-start.47 = (bf16[144,1728]{1,0:T(8,128)(2,1)S(1)}, bf16[144,1728]{1,0:T(8,128)(2,1)S(1)}, u32[]{:S(2)}, u32[]{:S(2)}) collective-permute-start(bf16[144,1728]{1,0:T(8,128)(2,1)S(1)} %get-tuple-element.147), channel_id=1, source_target_pairs={{0,24},{4,28},{8,0},{12,4},{16,8},{20,12},{24,16},{28,20},{1,25},{... | collective-permute-start | bytes 1493000 | tf_op jit(solution)/shard_map/ppermute | solution.py:23
  547.6 73.4 %collective-permute-start.46 = (bf16[144,1728]{1,0:T(8,128)(2,1)S(1)}, bf16[144,1728]{1,0:T(8,128)(2,1)S(1)}, u32[]{:S(2)}, u32[]{:S(2)}) collective-permute-start(bf16[144,1728]{1,0:T(8,128)(2,1)S(1)} %get-tuple-element.148), channel_id=1, source_target_pairs={{0,16},{4,20},{8,24},{12,28},{16,0},{20,4},{24,8},{28,12},{1,17},{... | collective-permute-start | bytes 1493000 | tf_op jit(solution)/shard_map/ppermute | solution.py:23
  549.6 71.4 %collective-permute-start.45 = (bf16[144,1728]{1,0:T(8,128)(2,1)S(1)}, bf16[144,1728]{1,0:T(8,128)(2,1)S(1)}, u32[]{:S(2)}, u32[]{:S(2)}) collective-permute-start(bf16[144,1728]{1,0:T(8,128)(2,1)S(1)} %get-tuple-element.146), channel_id=1, source_target_pairs={{0,8},{4,12},{8,16},{12,20},{16,24},{20,28},{24,0},{28,4},{1,9},{5... | collective-permute-start | bytes 1493000 | tf_op jit(solution)/shard_map/ppermute | solution.py:23
  584.9 37.3 %collective-permute-start.40 = (bf16[144,1152]{1,0:T(8,128)(2,1)S(1)}, bf16[144,1152]{1,0:T(8,128)(2,1)S(1)}, u32[]{:S(2)}, u32[]{:S(2)}) collective-permute-start(bf16[144,1152]{1,0:T(8,128)(2,1)S(1)} %get-tuple-element.150), channel_id=1, source_target_pairs={{0,24},{4,28},{8,0},{12,4},{16,8},{20,12},{24,16},{28,20},{1,25},{... | collective-permute-start | bytes 995336 | tf_op jit(solution)/shard_map/ppermute | solution.py:23
  585.0 58.8 %collective-permute-start.39 = (bf16[144,1152]{1,0:T(8,128)(2,1)S(1)}, bf16[144,1152]{1,0:T(8,128)(2,1)S(1)}, u32[]{:S(2)}, u32[]{:S(2)}) collective-permute-start(bf16[144,1152]{1,0:T(8,128)(2,1)S(1)} %get-tuple-element.151), channel_id=1, source_target_pairs={{0,16},{4,20},{8,24},{12,28},{16,0},{20,4},{24,8},{28,12},{1,17},{... | collective-permute-start | bytes 995336 | tf_op jit(solution)/shard_map/ppermute | solution.py:23
  586.9 56.8 %collective-permute-start.38 = (bf16[144,1152]{1,0:T(8,128)(2,1)S(1)}, bf16[144,1152]{1,0:T(8,128)(2,1)S(1)}, u32[]{:S(2)}, u32[]{:S(2)}) collective-permute-start(bf16[144,1152]{1,0:T(8,128)(2,1)S(1)} %get-tuple-element.149), channel_id=1, source_target_pairs={{0,8},{4,12},{8,16},{12,20},{16,24},{20,28},{24,0},{28,4},{1,9},{5... | collective-permute-start | bytes 995336 | tf_op jit(solution)/shard_map/ppermute | solution.py:23
  (101 other events, 1556.3 us)
Sparse Core Ops, SparseCore 0:
  10.2 172.9 all-gather.1
  399.1 108.8 reduce-scatter.8
  512.0 125.6 reduce-scatter.6

commit v3 on v2

--- a/solution.py
+++ b/solution.py
@@ -61,24 +61,6 @@
 def swap_pairs(value):
     count = lax.axis_size("dp")
     return lax.ppermute(value, "dp", [(i, i + 1 - 2 * (i % 2)) for i in range(count)])
-
-
-def gather_dp(value):
-    half = lax.axis_size("dp") // 2
-    me = lax.axis_index("dp")
-    other = swap_pairs(value)
-    pair = jnp.where(
-        lax.rem(me, 2) == 0,
-        jnp.concatenate([value, other], axis=0),
-        jnp.concatenate([other, value], axis=0),
-    )
-    rows = pair.shape[0]
-    whole = jnp.zeros((half * rows,) + value.shape[1:], value.dtype)
-    for step in range(half):
-        block = pair if step == 0 else shifted(pair, "dp", -2 * step)
-        owner = lax.rem(me // 2 + step, half)
-        whole = lax.dynamic_update_slice_in_dim(whole, block, owner * rows, axis=0)
-    return whole
 
 
 def scatter_dp(value):
@@ -178,9 +160,9 @@
     packed = jnp.concatenate(
         [q_weight, kv_weight, jnp.transpose(o_weight), gain_columns], axis=1
     )
-    packed_full = gather_dp(packed)
+    packed_full = lax.all_gather(packed, "dp", axis=0, tiled=True)
     gate_up_full = lax.all_gather(gate_up_weight, "dp", axis=1, tiled=True)
-    down_turned = gather_dp(jnp.transpose(down_weight))
+    down_full = lax.all_gather(down_weight, "dp", axis=1, tiled=True)
     joint_weight = packed_full[:, : 3 * head_size]
     output_turned = packed_full[:, 3 * head_size : 4 * head_size]
     gain_block = jnp.transpose(packed_full[:, 4 * head_size :]).astype(jnp.float32)
@@ -253,9 +235,7 @@
     hidden = gated_units(gate, up_part).astype(jnp.bfloat16)
     ff_out = scatter_relative(
         split_rows(
-            jnp.einsum(
-                "lf,df->ld", hidden, down_turned, preferred_element_type=jnp.float32
-            ).astype(jnp.bfloat16)
+            jnp.dot(hidden, down_full, preferred_element_type=jnp.float32).astype(jnp.bfloat16)
         )
     )
     result = (middle + normalize(ff_out, gains[3])).astype(jnp.bfloat16)
@@ -267,7 +247,7 @@
     ).astype(jnp.bfloat16)
     ff_grad_all, down_low = lax.optimization_barrier((ff_grad_all, down_low))
     hidden_grad = jnp.einsum(
-        "ld,df->lf", ff_grad_all, down_turned, preferred_element_type=jnp.float32
+        "ld,fd->lf", ff_grad_all, down_full, preferred_element_type=jnp.float32
     )
     unused, unit_pull = jax.vjp(gated_units, gate, up_part)
     gate_grad, up_grad = unit_pull(hidden_grad)

time: 684 us -> 633 us (0.925)
  local copies, waits for them, and re-layouts: 139 us -> 67.1 us
  waiting for transfers between devices: 346 us -> 409 us
  starting transfers between devices: 73.1 us -> 45.1 us
    all_gather x0 -> x2, waiting for transfers between devices: none -> 116 us  [the longest x1 59.2 us: local(): down_full = lax.all_gather(down_weight, 'dp', axis=1, tiled=True)]
    ppermute x39 -> x33, waiting for transfers between devices: 246 us -> 146 us  [shifted(): lax.ppermute(value, axis, [(i, (i + shift) % count) for i in range(count)])]
    all_gather x1, waiting for transfers between devices: 0.01 us -> 54.7 us  [local(): gate_up_full = lax.all_gather(gate_up_weight, 'dp', axis=1, tiled=True)]
    dynamic_update_slice x7 -> x0, local copies, waits for them, and re-layouts: 48.4 us -> none  [gather_dp(): whole = lax.dynamic_update_slice_in_dim(whole, block, owner * rows, axis=0)]
    ppermute x39 -> x33, starting transfers between devices: 55.8 us -> 24.8 us  [shifted(): lax.ppermute(value, axis, [(i, (i + shift) % count) for i in range(count)])]
    ppermute x4 -> x2, waiting for transfers between devices: 43.2 us -> 33.4 us  [swap_pairs(): lax.ppermute(value, 'dp', [(i, i + 1 - 2 * (i % 2)) for i in range(count)])]
    dot_general x2, matrix products: 21 us -> 13.1 us  [the longest x1 7.83 us: local(): jnp.einsum('ld,fd->lf', ff_grad_all, down_full, preferred_element_type=jn...]
    ppermute x5, starting transfers between devices: 12.5 us -> 19.4 us  [from_behind(): lax.ppermute(value, axis, [(source, source + steps) for source in range(l...]
  transfers between devices with their start and end apart: 51 -> 45, of which waited for: 24 -> 32; matrix products, arithmetic and copies ran while one was open for 24% -> 15% of each run, Pallas kernels for 0% -> 0%
where the time goes in v3:
time: 633 us; the launch traced here: 625 us
  waiting for transfers between devices  409 us (65%)
  local copies, waits for them, and re-layouts  67.1 us (11%)
  matrix products  60.3 us (10%)
  starting transfers between devices  45.1 us (7%)
  other arithmetic  28.3 us (4%)
  between operations  15.5 us (2%)
    ppermute x33, waiting for transfers between devices, shifted(): lax.ppermute(value, axis, [(i, (i + shift) % count) for i in range(count)])  146 us
    all_gather x1, waiting for transfers between devices, local(): down_full = lax.all_gather(down_weight, 'dp', axis=1, tiled=True)  59.2 us
    ppermute x5, waiting for transfers between devices, from_behind(): lax.ppermute(value, axis, [(source, source + steps) for source in range(l...  57.7 us
    all_gather x1, waiting for transfers between devices, local(): packed_full = lax.all_gather(packed, 'dp', axis=0, tiled=True)  56.9 us
    all_gather x1, waiting for transfers between devices, local(): gate_up_full = lax.all_gather(gate_up_weight, 'dp', axis=1, tiled=True)  54.7 us
    ppermute x2, waiting for transfers between devices, swap_pairs(): lax.ppermute(value, 'dp', [(i, i + 1 - 2 * (i % 2)) for i in range(count)])  33.4 us
    unnamed x174, local copies, waits for them, and re-layouts  25.2 us
    ppermute x33, starting transfers between devices, shifted(): lax.ppermute(value, axis, [(i, (i + shift) % count) for i in range(count)])  24.8 us
  transfers between devices with their start and end apart: 45, of which 32 were waited for; matrix products, arithmetic and copies ran while one was open for 15% of the time, Pallas kernels for 0%

profile of v3, /device:TPU:0, one launch (start us, length us, event | category | flops | bytes accessed | tf_op | source)
XLA Modules:
  0.0 624.9 jit_solution(16964376070866755060)
XLA Ops:
  14.2 56.9 %all-gather.4.cloned.1.call-done = bf16[1152,1152]{1,0:T(8,128)(2,1)} async-done(((bf16[144,1152]{1,0:T(8,128)(2,1)}), bf16[1152,1152]{1,0:T(8,128)(2,1)}) %all-gather.4.cloned.1.call-update) | async-done | bytes 2654224 | tf_op jit(solution)/shard_map/all_gather | solution.py:163
  76.5 3.9 collective-permute-done.1
  80.4 9.1 %collective-permute-done.2 = bf16[128,1152]{1,0:T(8,128)(2,1)S(1)} collective-permute-done((bf16[128,1152]{1,0:T(8,128)(2,1)S(1)}, bf16[128,1152]{1,0:T(8,128)(2,1)S(1)}, u32[]{:S(2)}, u32[]{:S(2)}) %collective-permute-start.2) | collective-permute-done | bytes 294944 | tf_op jit(solution)/shard_map/ppermute | solution.py:23
  97.4 4.3 collective-permute-start
  103.1 10.1 %collective-permute-start.5 = (bf16[512,256]{1,0:T(8,128)(2,1)S(1)}, bf16[512,256]{1,0:T(8,128)(2,1)S(1)}, u32[]{:S(2)}, u32[]{:S(2)}) collective-permute-start(bf16[512,256]{1,0:T(8,128)(2,1)S(1)} %slice.328), channel_id=1, source_target_pairs={{0,4},{4,8},{8,12},{12,16},{16,20},{20,24},{24,28},{1,5},{5,9},{9,... | collective-permute-start | bytes 786440 | tf_op jit(solution)/shard_map/ppermute | solution.py:18
  120.8 5.7 collective-permute-done.8
  126.5 7.6 %collective-permute-done.7 = bf16[128,1152]{1,0:T(8,128)(2,1)S(1)} collective-permute-done((bf16[128,1152]{1,0:T(8,128)(2,1)S(1)}, bf16[128,1152]{1,0:T(8,128)(2,1)S(1)}, u32[]{:S(2)}, u32[]{:S(2)}) %collective-permute-start.7) | collective-permute-done | bytes 294944 | tf_op jit(solution)/shard_map/ppermute | solution.py:23
  138.2 6.0 collective-permute-done.11
  149.7 54.7 %all-gather.6.cloned.1.call-done = bf16[2,1152,1728]{2,1,0:T(8,128)(2,1)} async-done(((bf16[2,144,1728]{2,1,0:T(8,128)(2,1)}), bf16[2,1152,1728]{2,1,0:T(8,128)(2,1)}) %all-gather.6.cloned.1.call-update) | async-done | bytes 7962640 | tf_op jit(solution)/shard_map/all_gather | solution.py:164
  204.4 5.2 fusion.2
  211.5 6.8 %multiply_convert_fusion.1 = (bf16[512,1728]{0,1:T(8,128)(2,1)}, f32[512,1728]{0,1:T(8,128)}) fusion(f32[512,1728]{0,1:T(8,128)S(1)} %fusion.2, bf16[2,1152,1728]{2,1,0:T(8,128)(2,1)S(1)} %copy-done.69, bf16[128,1152]{1,0:T(8,128)(2,1)S(1)} %copy-done.72, bf16[128,1152]{1,0:T(8,128)(2,1)S(1)} %copy-done.75, bf16[128,1152]{1,0:T(8,128)(2,1)} %collective-permute-done.9, ...), kind=kOutput, calls=%fused_computation.22 | convolution fusion | flops 2051997696 | bytes 14155776 | tf_op jit(solution)/shard_map/dot_general | solution.py:234
  218.2 59.2 %all-gather.8.cloned.1.call-done = bf16[1728,1152]{0,1:T(8,128)(2,1)} async-done(((bf16[1728,144]{0,1:T(8,128)(2,1)}), bf16[1728,1152]{0,1:T(8,128)(2,1)}) %all-gather.8.cloned.1.call-update) | async-done | bytes 3981328 | tf_op jit(solution)/shard_map/all_gather | solution.py:165
  277.4 5.3 convolution_convert_fusion.5
  284.6 4.7 collective-permute-done.14
  289.2 9.2 %collective-permute-done.13 = bf16[128,1152]{1,0:T(8,128)(2,1)S(1)} collective-permute-done((bf16[128,1152]{1,0:T(8,128)(2,1)S(1)}, bf16[128,1152]{1,0:T(8,128)(2,1)S(1)}, u32[]{:S(2)}, u32[]{:S(2)}) %collective-permute-start.13) | collective-permute-done | bytes 294944 | tf_op jit(solution)/shard_map/ppermute | solution.py:23
  302.6 6.7 %collective-permute-done.17 = bf16[128,1152]{1,0:T(8,128)(2,1)S(1)} collective-permute-done((bf16[128,1152]{1,0:T(8,128)(2,1)S(1)}, bf16[128,1152]{1,0:T(8,128)(2,1)S(1)}, u32[]{:S(2)}, u32[]{:S(2)}) %collective-permute-start.17) | collective-permute-done | bytes 294944 | tf_op jit(solution)/shard_map/ppermute | solution.py:23
  310.4 3.8 collective-permute-done.15
  314.4 4.5 convolution_convert_fusion.2
  318.9 7.8 %multiply_convert_fusion = (bf16[512,1728]{0,1:T(8,128)(2,1)S(1)}, bf16[512,1728]{0,1:T(8,128)(2,1)S(1)}) fusion(f32[512,1728]{0,1:T(8,128)S(1)} %copy-done.80, f32[512,1728]{0,1:T(8,128)} %get-tuple-element.185, bf16[512,1152]{1,0:T(8,128)(2,1)S(1)} %pad_maximum_fusion.1, bf16[1728,1152]{0,1:T(8,128)(2,1)S(1)} %copy-done.70), kind=kOutput, calls=%fused_computation.21 | convolution fusion | flops 2059665408 | bytes 15777792 | tf_op jit(solution)/shard_map/ld,fd->lf/dot_general | solution.py:249
  329.4 5.3 convolution_convert_fusion.1
  334.7 5.4 convolution_convert_fusion
  340.1 3.7 fusion.13
  343.8 6.5 %copy.58 = bf16[1152,1728]{1,0:T(8,128)(2,1)} copy(bf16[1152,1728]{0,1:T(8,128)(2,1)} %convolution_convert_fusion) | data formatting | bytes 7962624
  355.8 6.2 collective-permute-done.20
  362.0 7.8 %collective-permute-done.19 = bf16[128,1152]{1,0:T(8,128)(2,1)} collective-permute-done((bf16[128,1152]{1,0:T(8,128)(2,1)}, bf16[128,1152]{1,0:T(8,128)(2,1)}, u32[]{:S(2)}, u32[]{:S(2)}) %collective-permute-start.19) | collective-permute-done | bytes 294944 | tf_op jit(solution)/shard_map/ppermute | solution.py:23
  377.8 6.7 %copy.51 = bf16[1152,1728]{1,0:T(8,128)(2,1)} copy(bf16[1152,1728]{0,1:T(8,128)(2,1)} %convolution_convert_fusion.2) | data formatting | bytes 7962624 | tf_op jit(solution)/shard_map/optimization_barrier | solution.py:248
  388.1 6.5 %copy.56 = bf16[1152,1728]{1,0:T(8,128)(2,1)} copy(bf16[1152,1728]{0,1:T(8,128)(2,1)} %convolution_convert_fusion.1) | data formatting | bytes 7962624
  410.5 54.1 %collective-permute-done.24 = bf16[512,256]{1,0:T(8,128)(2,1)S(1)} collective-permute-done((bf16[512,256]{1,0:T(8,128)(2,1)S(1)}, bf16[512,256]{1,0:T(8,128)(2,1)S(1)}, u32[]{:S(2)}, u32[]{:S(2)}) %collective-permute-start.24) | collective-permute-done | bytes 262176 | tf_op jit(solution)/shard_map/ppermute | solution.py:18
  502.3 33.4 %collective-permute-done.29 = bf16[4,144,1152]{2,1,0:T(8,128)(2,1)S(1)} collective-permute-done((bf16[4,144,1152]{2,1,0:T(8,128)(2,1)S(1)}, bf16[4,144,1152]{2,1,0:T(8,128)(2,1)S(1)}, u32[]{:S(2)}, u32[]{:S(2)}) %collective-permute-start.29) | collective-permute-done | bytes 1327136 | tf_op jit(solution)/shard_map/ppermute | solution.py:63
  540.3 34.2 %collective-permute-done.38 = bf16[144,1728]{1,0:T(8,128)(2,1)S(1)} collective-permute-done((bf16[144,1728]{1,0:T(8,128)(2,1)S(1)}, bf16[144,1728]{1,0:T(8,128)(2,1)S(1)}, u32[]{:S(2)}, u32[]{:S(2)}) %collective-permute-start.38) | collective-permute-done | bytes 497696 | tf_op jit(solution)/shard_map/ppermute | solution.py:23
  575.8 20.1 %collective-permute-done.31 = bf16[144,1152]{1,0:T(8,128)(2,1)S(1)} collective-permute-done((bf16[144,1152]{1,0:T(8,128)(2,1)S(1)}, bf16[144,1152]{1,0:T(8,128)(2,1)S(1)}, u32[]{:S(2)}, u32[]{:S(2)}) %collective-permute-start.31) | collective-permute-done | bytes 331808 | tf_op jit(solution)/shard_map/ppermute | solution.py:23
  601.4 5.6 collective-permute-done.34
  (367 shorter events, 142.5 us)
Async XLA Ops:
  7.2 63.9 %all-gather.4.cloned.1.call-start = ((), (), s32[]{:S(2)}) async-start(), calls=%async_computation.2 | async-start | bytes 2985984 | tf_op jit(solution)/shard_map/all_gather | solution.py:163
  13.2 191.2 %all-gather.6.cloned.1.call-start = ((), (), s32[]{:S(2)}) async-start(), calls=%async_computation.3 | async-start | bytes 9289728 | tf_op jit(solution)/shard_map/all_gather | solution.py:164
  13.9 263.5 %all-gather.8.cloned.1.call-start = ((), (), s32[]{:S(2)}) async-start(), calls=%async_computation.4 | async-start | bytes 4644864 | tf_op jit(solution)/shard_map/all_gather | solution.py:165
  74.2 535.2 %reduce-scatter.9.cloned.1.call-start = ((), (), s32[]{:S(2)}) async-start(), calls=%async_computation.6 | async-start | bytes 4644864
  74.5 15.0 %collective-permute-start.2 = (bf16[128,1152]{1,0:T(8,128)(2,1)S(1)}, bf16[128,1152]{1,0:T(8,128)(2,1)S(1)}, u32[]{:S(2)}, u32[]{:S(2)}) collective-permute-start(bf16[128,1152]{1,0:T(8,128)(2,1)S(1)} %get-tuple-element.141), channel_id=1, source_target_pairs={{0,2},{1,3},{2,0},{3,1},{4,6},{5,7},{6,4},{7,5},{8,10},{9,11},{10,... | collective-permute-start | bytes 884744 | tf_op jit(solution)/shard_map/ppermute | solution.py:23
  76.0 13.8 %collective-permute-start.3 = (bf16[128,1152]{1,0:T(8,128)(2,1)S(1)}, bf16[128,1152]{1,0:T(8,128)(2,1)S(1)}, u32[]{:S(2)}, u32[]{:S(2)}) collective-permute-start(bf16[128,1152]{1,0:T(8,128)(2,1)S(1)} %get-tuple-element.141), channel_id=1, source_target_pairs={{0,1},{1,2},{2,3},{3,0},{4,5},{5,6},{6,7},{7,4},{8,9},{9,10},{10,1... | collective-permute-start | bytes 884744 | tf_op jit(solution)/shard_map/ppermute | solution.py:23
  94.9 18.2 %collective-permute-start.4 = (bf16[512,256]{1,0:T(8,128)(2,1)S(1)}, bf16[512,256]{1,0:T(8,128)(2,1)S(1)}, u32[]{:S(2)}, u32[]{:S(2)}) collective-permute-start(bf16[512,256]{1,0:T(8,128)(2,1)S(1)} %pad_maximum_fusion.9), channel_id=1, source_target_pairs={{0,4},{4,8},{8,12},{12,16},{16,20},{20,24},{24,28},{1,5},{5,9},{9,... | collective-permute-start | bytes 786440 | tf_op jit(solution)/shard_map/ppermute | solution.py:18
  103.1 13.9 %collective-permute-start.5 = (bf16[512,256]{1,0:T(8,128)(2,1)S(1)}, bf16[512,256]{1,0:T(8,128)(2,1)S(1)}, u32[]{:S(2)}, u32[]{:S(2)}) collective-permute-start(bf16[512,256]{1,0:T(8,128)(2,1)S(1)} %slice.328), channel_id=1, source_target_pairs={{0,4},{4,8},{8,12},{12,16},{16,20},{20,24},{24,28},{1,5},{5,9},{9,... | collective-permute-start | bytes 786440 | tf_op jit(solution)/shard_map/ppermute | solution.py:18
  119.6 14.6 %collective-permute-start.7 = (bf16[128,1152]{1,0:T(8,128)(2,1)S(1)}, bf16[128,1152]{1,0:T(8,128)(2,1)S(1)}, u32[]{:S(2)}, u32[]{:S(2)}) collective-permute-start(bf16[128,1152]{1,0:T(8,128)(2,1)S(1)} %get-tuple-element.165), channel_id=1, source_target_pairs={{0,2},{1,3},{2,0},{3,1},{4,6},{5,7},{6,4},{7,5},{8,10},{9,11},{10,... | collective-permute-start | bytes 884744 | tf_op jit(solution)/shard_map/ppermute | solution.py:23
  120.6 14.1 %collective-permute-start.6 = (bf16[128,1152]{1,0:T(8,128)(2,1)S(1)}, bf16[128,1152]{1,0:T(8,128)(2,1)S(1)}, u32[]{:S(2)}, u32[]{:S(2)}) collective-permute-start(bf16[128,1152]{1,0:T(8,128)(2,1)S(1)} %get-tuple-element.163), channel_id=1, source_target_pairs={{0,1},{1,2},{2,3},{3,0},{4,5},{5,6},{6,7},{7,4},{8,9},{9,10},{10,1... | collective-permute-start | bytes 884744 | tf_op jit(solution)/shard_map/ppermute | solution.py:23
  136.7 13.1 %collective-permute-start.9 = (bf16[128,1152]{1,0:T(8,128)(2,1)S(1)}, bf16[128,1152]{1,0:T(8,128)(2,1)}, u32[]{:S(2)}, u32[]{:S(2)}) collective-permute-start(bf16[128,1152]{1,0:T(8,128)(2,1)S(1)} %multiply_convert_fusion.3), channel_id=1, source_target_pairs={{0,3},{1,0},{2,1},{3,2},{4,7},{5,4},{6,5},{7,6},{8,11},{9,8},{10,9... | collective-permute-start | bytes 884744 | tf_op jit(solution)/shard_map/ppermute | solution.py:23
  282.9 15.5 %collective-permute-start.13 = (bf16[128,1152]{1,0:T(8,128)(2,1)S(1)}, bf16[128,1152]{1,0:T(8,128)(2,1)S(1)}, u32[]{:S(2)}, u32[]{:S(2)}) collective-permute-start(bf16[128,1152]{1,0:T(8,128)(2,1)S(1)} %get-tuple-element.162), channel_id=1, source_target_pairs={{0,2},{1,3},{2,0},{3,1},{4,6},{5,7},{6,4},{7,5},{8,10},{9,11},{10,... | collective-permute-start | bytes 884744 | tf_op jit(solution)/shard_map/ppermute | solution.py:23
  284.4 14.1 %collective-permute-start.12 = (bf16[128,1152]{1,0:T(8,128)(2,1)S(1)}, bf16[128,1152]{1,0:T(8,128)(2,1)S(1)}, u32[]{:S(2)}, u32[]{:S(2)}) collective-permute-start(bf16[128,1152]{1,0:T(8,128)(2,1)S(1)} %get-tuple-element.160), channel_id=1, source_target_pairs={{0,1},{1,2},{2,3},{3,0},{4,5},{5,6},{6,7},{7,4},{8,9},{9,10},{10,1... | collective-permute-start | bytes 884744 | tf_op jit(solution)/shard_map/ppermute | solution.py:23
  301.1 13.1 %collective-permute-start.15 = (bf16[128,1152]{1,0:T(8,128)(2,1)S(1)}, bf16[128,1152]{1,0:T(8,128)(2,1)S(1)}, u32[]{:S(2)}, u32[]{:S(2)}) collective-permute-start(bf16[128,1152]{1,0:T(8,128)(2,1)S(1)} %get-tuple-element.168), channel_id=1, source_target_pairs={{0,3},{1,0},{2,1},{3,2},{4,7},{5,4},{6,5},{7,6},{8,11},{9,8},{10,9... | collective-permute-start | bytes 884744 | tf_op jit(solution)/shard_map/ppermute | solution.py:23
  350.3 261.4 %reduce-scatter.7.cloned.1.call-start = ((), (), s32[]{:S(2)}) async-start(), calls=%async_computation.5 | async-start | bytes 4644864
  354.4 15.4 %collective-permute-start.19 = (bf16[128,1152]{1,0:T(8,128)(2,1)}, bf16[128,1152]{1,0:T(8,128)(2,1)}, u32[]{:S(2)}, u32[]{:S(2)}) collective-permute-start(bf16[128,1152]{1,0:T(8,128)(2,1)} %get-tuple-element.159), channel_id=1, source_target_pairs={{0,2},{1,3},{2,0},{3,1},{4,6},{5,7},{6,4},{7,5},{8,10},{9,11},{10,... | collective-permute-start | bytes 884744 | tf_op jit(solution)/shard_map/ppermute | solution.py:23
  355.8 14.0 %collective-permute-start.18 = (bf16[128,1152]{1,0:T(8,128)(2,1)}, bf16[128,1152]{1,0:T(8,128)(2,1)}, u32[]{:S(2)}, u32[]{:S(2)}) collective-permute-start(bf16[128,1152]{1,0:T(8,128)(2,1)} %get-tuple-element.157), channel_id=1, source_target_pairs={{0,1},{1,2},{2,3},{3,0},{4,5},{5,6},{6,7},{7,4},{8,9},{9,10},{10,1... | collective-permute-start | bytes 884744 | tf_op jit(solution)/shard_map/ppermute | solution.py:23
  377.2 20.2 %collective-permute-start.21 = (bf16[128,1152]{1,0:T(8,128)(2,1)}, bf16[128,1152]{1,0:T(8,128)(2,1)}, u32[]{:S(2)}, u32[]{:S(2)}) collective-permute-start(bf16[128,1152]{1,0:T(8,128)(2,1)} %get-tuple-element.132), channel_id=1, source_target_pairs={{0,3},{1,0},{2,1},{3,2},{4,7},{5,4},{6,5},{7,6},{8,11},{9,8},{10,9... | collective-permute-start | bytes 884744 | tf_op jit(solution)/shard_map/ppermute | solution.py:23
  384.5 13.8 %collective-permute-start.22 = (bf16[128,1152]{1,0:T(8,128)(2,1)}, bf16[128,1152]{1,0:T(8,128)(2,1)}, u32[]{:S(2)}, u32[]{:S(2)}) collective-permute-start(bf16[128,1152]{1,0:T(8,128)(2,1)} %get-tuple-element.132), channel_id=1, source_target_pairs={{0,2},{1,3},{2,0},{3,1},{4,6},{5,7},{6,4},{7,5},{8,10},{9,11},{10,... | collective-permute-start | bytes 884744 | tf_op jit(solution)/shard_map/ppermute | solution.py:23
  394.6 101.5 %collective-permute-start.36 = (bf16[4,144,1728]{2,1,0:T(8,128)(2,1)}, bf16[4,144,1728]{2,1,0:T(8,128)(2,1)}, u32[]{:S(2)}, u32[]{:S(2)}) collective-permute-start(bf16[4,144,1728]{2,1,0:T(8,128)(2,1)} %dynamic-slice_bitcast_fusion), channel_id=1, source_target_pairs={{0,4},{4,0},{8,12},{12,8},{16,20},{20,16},{24,28},{28,24},{1,5},{5... | collective-permute-start | bytes 5971976 | tf_op jit(solution)/shard_map/ppermute | solution.py:63
  405.2 61.7 %collective-permute-start.25 = (bf16[512,256]{1,0:T(8,128)(2,1)S(1)}, bf16[512,256]{1,0:T(8,128)(2,1)S(1)}, u32[]{:S(2)}, u32[]{:S(2)}) collective-permute-start(bf16[512,256]{1,0:T(8,128)(2,1)S(1)} %slice.326), channel_id=1, source_target_pairs={{4,0},{8,4},{12,8},{16,12},{20,16},{24,20},{28,24},{5,1},{9,5},{13... | collective-permute-start | bytes 786440 | tf_op jit(solution)/shard_map/ppermute | solution.py:18
  408.7 56.0 %collective-permute-start.24 = (bf16[512,256]{1,0:T(8,128)(2,1)S(1)}, bf16[512,256]{1,0:T(8,128)(2,1)S(1)}, u32[]{:S(2)}, u32[]{:S(2)}) collective-permute-start(bf16[512,256]{1,0:T(8,128)(2,1)S(1)} %slice.327), channel_id=1, source_target_pairs={{4,0},{8,4},{12,8},{16,12},{20,16},{24,20},{28,24},{5,1},{9,5},{13... | collective-permute-start | bytes 786440 | tf_op jit(solution)/shard_map/ppermute | solution.py:18
  468.7 12.4 %collective-permute-start.28 = (bf16[128,1152]{1,0:T(8,128)(2,1)S(1)}, bf16[128,1152]{1,0:T(8,128)(2,1)S(1)}, u32[]{:S(2)}, u32[]{:S(2)}) collective-permute-start(bf16[128,1152]{1,0:T(8,128)(2,1)S(1)} %get-tuple-element.155), channel_id=1, source_target_pairs={{0,3},{1,0},{2,1},{3,2},{4,7},{5,4},{6,5},{7,6},{8,11},{9,8},{10,9... | collective-permute-start | bytes 884744 | tf_op jit(solution)/shard_map/ppermute | solution.py:23
  469.2 15.0 %collective-permute-start.27 = (bf16[128,1152]{1,0:T(8,128)(2,1)S(1)}, bf16[128,1152]{1,0:T(8,128)(2,1)S(1)}, u32[]{:S(2)}, u32[]{:S(2)}) collective-permute-start(bf16[128,1152]{1,0:T(8,128)(2,1)S(1)} %get-tuple-element.156), channel_id=1, source_target_pairs={{0,2},{1,3},{2,0},{3,1},{4,6},{5,7},{6,4},{7,5},{8,10},{9,11},{10,... | collective-permute-start | bytes 884744 | tf_op jit(solution)/shard_map/ppermute | solution.py:23
  470.1 14.3 %collective-permute-start.26 = (bf16[128,1152]{1,0:T(8,128)(2,1)S(1)}, bf16[128,1152]{1,0:T(8,128)(2,1)}, u32[]{:S(2)}, u32[]{:S(2)}) collective-permute-start(bf16[128,1152]{1,0:T(8,128)(2,1)S(1)} %get-tuple-element.154), channel_id=1, source_target_pairs={{0,1},{1,2},{2,3},{3,0},{4,5},{5,6},{6,7},{7,4},{8,9},{9,10},{10,1... | collective-permute-start | bytes 884744 | tf_op jit(solution)/shard_map/ppermute | solution.py:23
  495.0 40.7 %collective-permute-start.29 = (bf16[4,144,1152]{2,1,0:T(8,128)(2,1)S(1)}, bf16[4,144,1152]{2,1,0:T(8,128)(2,1)S(1)}, u32[]{:S(2)}, u32[]{:S(2)}) collective-permute-start(bf16[4,144,1152]{2,1,0:T(8,128)(2,1)S(1)} %dynamic-slice_bitcast_fusion.1), channel_id=1, source_target_pairs={{0,4},{4,0},{8,12},{12,8},{16,20},{20,16},{24,28},{28,24},{1,5},{5... | collective-permute-start | bytes 3981320 | tf_op jit(solution)/shard_map/ppermute | solution.py:63
  498.4 40.0 %collective-permute-start.39 = (bf16[144,1728]{1,0:T(8,128)(2,1)S(1)}, bf16[144,1728]{1,0:T(8,128)(2,1)S(1)}, u32[]{:S(2)}, u32[]{:S(2)}) collective-permute-start(bf16[144,1728]{1,0:T(8,128)(2,1)S(1)} %get-tuple-element.145), channel_id=1, source_target_pairs={{0,24},{4,28},{8,0},{12,4},{16,8},{20,12},{24,16},{28,20},{1,25},{... | collective-permute-start | bytes 1493000 | tf_op jit(solution)/shard_map/ppermute | solution.py:23
  500.4 74.2 %collective-permute-start.38 = (bf16[144,1728]{1,0:T(8,128)(2,1)S(1)}, bf16[144,1728]{1,0:T(8,128)(2,1)S(1)}, u32[]{:S(2)}, u32[]{:S(2)}) collective-permute-start(bf16[144,1728]{1,0:T(8,128)(2,1)S(1)} %get-tuple-element.146), channel_id=1, source_target_pairs={{0,16},{4,20},{8,24},{12,28},{16,0},{20,4},{24,8},{28,12},{1,17},{... | collective-permute-start | bytes 1493000 | tf_op jit(solution)/shard_map/ppermute | solution.py:23
  501.0 73.5 %collective-permute-start.37 = (bf16[144,1728]{1,0:T(8,128)(2,1)S(1)}, bf16[144,1728]{1,0:T(8,128)(2,1)S(1)}, u32[]{:S(2)}, u32[]{:S(2)}) collective-permute-start(bf16[144,1728]{1,0:T(8,128)(2,1)S(1)} %get-tuple-element.144), channel_id=1, source_target_pairs={{0,8},{4,12},{8,16},{12,20},{16,24},{20,28},{24,0},{28,4},{1,9},{5... | collective-permute-start | bytes 1493000 | tf_op jit(solution)/shard_map/ppermute | solution.py:23
  536.1 39.6 %collective-permute-start.32 = (bf16[144,1152]{1,0:T(8,128)(2,1)S(1)}, bf16[144,1152]{1,0:T(8,128)(2,1)S(1)}, u32[]{:S(2)}, u32[]{:S(2)}) collective-permute-start(bf16[144,1152]{1,0:T(8,128)(2,1)S(1)} %get-tuple-element.148), channel_id=1, source_target_pairs={{0,24},{4,28},{8,0},{12,4},{16,8},{20,12},{24,16},{28,20},{1,25},{... | collective-permute-start | bytes 995336 | tf_op jit(solution)/shard_map/ppermute | solution.py:23
  536.4 59.5 %collective-permute-start.31 = (bf16[144,1152]{1,0:T(8,128)(2,1)S(1)}, bf16[144,1152]{1,0:T(8,128)(2,1)S(1)}, u32[]{:S(2)}, u32[]{:S(2)}) collective-permute-start(bf16[144,1152]{1,0:T(8,128)(2,1)S(1)} %get-tuple-element.149), channel_id=1, source_target_pairs={{0,16},{4,20},{8,24},{12,28},{16,0},{20,4},{24,8},{28,12},{1,17},{... | collective-permute-start | bytes 995336 | tf_op jit(solution)/shard_map/ppermute | solution.py:23
  538.4 57.5 %collective-permute-start.30 = (bf16[144,1152]{1,0:T(8,128)(2,1)S(1)}, bf16[144,1152]{1,0:T(8,128)(2,1)S(1)}, u32[]{:S(2)}, u32[]{:S(2)}) collective-permute-start(bf16[144,1152]{1,0:T(8,128)(2,1)S(1)} %get-tuple-element.147), channel_id=1, source_target_pairs={{0,8},{4,12},{8,16},{12,20},{16,24},{20,28},{24,0},{28,4},{1,9},{5... | collective-permute-start | bytes 995336 | tf_op jit(solution)/shard_map/ppermute | solution.py:23
  (98 other events, 1162.3 us)
Sparse Core Ops, SparseCore 0:
  13.3 57.7 all-gather.3
  73.3 131.1 all-gather.5
  206.6 70.7 all-gather.7
  350.5 109.9 reduce-scatter.8
  464.3 123.9 reduce-scatter.6
